TPU v7x, 32 devices: a whole 2x2x4 slice. The times are simulated.
32 devices in a mesh: groups: 2 (over y), seq: 4 (over z), section: 2 (over x), chan: 2 (over core).
Axes of the slice: x: 2, y: 2, z: 4, core: 2. Of those that a mesh axis runs over, the one named last changes fastest.
Arguments:
- base_codes: int32 [131072], P(('groups', 'seq', 'section')), parts along dimension 0, may hold values from 0 to 3
- stem_weight: bfloat16 [64, 768], replicated, as said below
- conv_gain: float32 [768], replicated, may hold values from 0.1 to 1.9
- dilated_conv_weight: bfloat16 [3, 768, 768], P(None, None, 'chan'), may hold values from -0.125 to 0.125
- widen_weight: bfloat16 [768, 1536], P(None, 'chan'), may hold values from -0.21875 to 0.21875
- token_gain: float32 [1536], replicated, may hold values from 0.1 to 1.9
- proj_weight: bfloat16 [1536, 256], replicated, may hold values from -0.15625 to 0.15625
- dist_weight: float32 [128], replicated, may hold values from -4 to 4
- pair_weight_one: bfloat16 [3, 3, 128, 128], P(None, None, None, 'chan'), may hold values from -0.1875 to 0.1875
- pair_weight_two: bfloat16 [3, 3, 128, 128], P(None, None, None, 'chan'), may hold values from -0.1875 to 0.1875
Outputs:
- fine_features: bfloat16 [4096, 1536], P(('groups', 'seq', 'section'), 'chan'), parts along dimension 0
- pair_map: bfloat16 [128, 64, 32], P('chan', ('groups', 'seq'), 'section'), parts along dimension 1
There are 2 independent parts, one for each index of `groups`. A program takes and returns all parts, laid end to end along the dimension named above; an argument that names none is the same for every part. Nothing has to cross between parts.
Inputs may be any that keep to these rules, and one draw needn't show every extreme that they name: Each entry of stem_weight is under 9 / sqrt(16) in magnitude.
All inputs are finite; a program needn't handle non-finite values.
Results may differ from a plain program's by a relative error of at most 0.015.
Values may be sent and summed in bfloat16 or wider, within the bound.
A program may use at most 64 MiB of HBM per device.

v0:
```python
import math

import jax
import jax.numpy as jnp
from jax import lax
from jax.sharding import PartitionSpec as P

PC = 128
PATCH = 16
POOL = 64
DILATION_ROWS = 4


epsilon = 1e-06


def padded(cells, sides, width):
    for axis, dim in sides:
        count = lax.axis_size(axis)
        ends = count - 1
        head = lax.slice_in_dim(cells, 0, width, axis=dim)
        tail = lax.slice_in_dim(cells, cells.shape[dim] - width, cells.shape[dim], axis=dim)
        cells = jnp.concatenate(
            [
                lax.ppermute(tail, axis, [(i, (i + 1) % count) for i in range(ends)]),
                cells,
                lax.ppermute(head, axis, [((i + 1) % count, i) for i in range(ends)]),
            ],
            axis=dim,
        )
    return cells


def row_norm(values, gain):
    mean_square = jnp.mean(values * values, axis=1, keepdims=True)
    return values * lax.rsqrt(mean_square + epsilon) * gain


def pair_conv(active, weight):
    row_len = active.shape[1] - 2
    col_len = active.shape[2] - 2
    total = jnp.zeros((weight.shape[3], row_len, col_len), jnp.float32)
    for shift_row in range(3):
        for shift_col in range(3):
            window = active[:, shift_row : shift_row + row_len, shift_col : shift_col + col_len]
            total = total + jnp.einsum(
                "co,crs->ors",
                weight[shift_row, shift_col],
                window,
                preferred_element_type=jnp.float32,
            )
    return total


def make_pair(row_factor, col_factor, row_index, col_index, dist_weight, tokens_total):
    gap = jnp.abs(row_index[:, None] - col_index[None, :]).astype(jnp.float32)
    distance = jnp.log1p(gap) / math.log(tokens_total)
    product = (
        row_factor.astype(jnp.float32).T[:, :, None] * col_factor.astype(jnp.float32).T[:, None, :]
    )
    return product + dist_weight[:, None, None] * distance[None, :, :]


def per_device(
    base_codes,
    stem_weight,
    conv_gain,
    dilated_conv_weight,
    widen_weight,
    token_gain,
    proj_weight,
    dist_weight,
    pair_weight_one,
    pair_weight_two,
):
    count_of_rows = base_codes.shape[0] // PATCH
    coded = base_codes.reshape(count_of_rows, PATCH)
    onehot = (
        (coded[:, :, None] == jnp.arange(4, dtype=jnp.int32)[None, None, :])
        .astype(jnp.bfloat16)
        .reshape(count_of_rows, 4 * PATCH)
    )
    half_width = dilated_conv_weight.shape[2]
    own_index = lax.axis_index("chan")
    weight_own = lax.dynamic_slice_in_dim(stem_weight, own_index * half_width, half_width, 1)
    stem_own = jnp.dot(onehot, weight_own, preferred_element_type=jnp.float32).astype(jnp.bfloat16)
    full_stem_output = lax.all_gather(stem_own, "chan", axis=1, tiled=True)
    padded_rows = padded(full_stem_output, ((("seq", "section"), 0),), DILATION_ROWS)
    normalized_rows = row_norm(padded_rows.astype(jnp.float32), conv_gain).astype(jnp.bfloat16)
    summed_taps = jnp.zeros((count_of_rows, half_width), jnp.float32)
    for row_shift_amount in range(3):
        summed_taps = summed_taps + jnp.dot(
            normalized_rows[
                row_shift_amount * DILATION_ROWS : row_shift_amount * DILATION_ROWS + count_of_rows
            ],
            dilated_conv_weight[row_shift_amount],
            preferred_element_type=jnp.float32,
        )
    tower = (stem_own.astype(jnp.float32) + jax.nn.gelu(summed_taps)).astype(jnp.bfloat16)
    halved = jnp.maximum(tower[0::2], tower[1::2])
    widened = jnp.dot(
        lax.all_gather(halved, "chan", axis=1, tiled=True),
        widen_weight,
        preferred_element_type=jnp.float32,
    )
    fine_features = jax.nn.gelu(widened).astype(jnp.bfloat16)
    tok_count = fine_features.shape[0] // POOL
    token = jnp.mean(
        fine_features.astype(jnp.float32).reshape(tok_count, POOL, fine_features.shape[1]), axis=1
    ).astype(jnp.bfloat16)
    token_full = lax.all_gather(token, "chan", axis=1, tiled=True)
    token_norm = row_norm(token_full.astype(jnp.float32), token_gain).astype(jnp.bfloat16)
    factors = jnp.dot(token_norm, proj_weight, preferred_element_type=jnp.float32).astype(
        jnp.bfloat16
    )
    seq_count = lax.axis_size("seq")
    section_count = lax.axis_size("section")
    tokens_total = tok_count * seq_count * section_count
    tile_height = tok_count * section_count
    tile_width = tok_count * seq_count
    row_anchor = lax.axis_index("seq") * tile_height
    col_anchor = lax.axis_index("section") * tile_width
    pair_own = pair_weight_one.shape[3]
    every_token = lax.all_gather(factors, ("seq", "section"), axis=0, tiled=True)
    zero_padded = jnp.pad(every_token, ((1, 1), (0, 0)))
    row_factor = lax.dynamic_slice_in_dim(zero_padded, row_anchor, tile_height + 2, 0)[:, :PC]
    col_factor = lax.dynamic_slice_in_dim(zero_padded, col_anchor, tile_width + 2, 0)[:, PC:]
    row_index = row_anchor - 1 + jnp.arange(tile_height + 2, dtype=jnp.int32)
    col_index = col_anchor - 1 + jnp.arange(tile_width + 2, dtype=jnp.int32)
    extended = make_pair(
        row_factor, col_factor, row_index, col_index, dist_weight, tokens_total
    ).astype(jnp.bfloat16)
    row_valid = (row_index >= 0) & (row_index < tokens_total)
    col_valid = (col_index >= 0) & (col_index < tokens_total)
    inside = row_valid[:, None] & col_valid[None, :]
    act_one = jnp.where(inside[None, :, :], jax.nn.gelu(extended.astype(jnp.float32)), 0.0).astype(
        jnp.bfloat16
    )
    pair_start = extended[:, 1:-1, 1:-1]
    start_own = lax.dynamic_slice_in_dim(pair_start, own_index * pair_own, pair_own, 0)
    pair_mid = (start_own.astype(jnp.float32) + pair_conv(act_one, pair_weight_one)).astype(
        jnp.bfloat16
    )
    mid_full = lax.all_gather(pair_mid, "chan", axis=0, tiled=True)
    act_local_two = jax.nn.gelu(mid_full.astype(jnp.float32)).astype(jnp.bfloat16)
    act_two = padded(act_local_two, (("seq", 1), ("section", 2)), 1)
    pair_map = (pair_mid.astype(jnp.float32) + pair_conv(act_two, pair_weight_two)).astype(
        jnp.bfloat16
    )
    return (fine_features, pair_map)


def solution(mesh):
    in_specs = (
        P(("groups", "seq", "section")),
        P(),
        P(),
        P(None, None, "chan"),
        P(None, "chan"),
        P(),
        P(),
        P(),
        P(None, None, None, "chan"),
        P(None, None, None, "chan"),
    )
    out_specs = (P(("groups", "seq", "section"), "chan"), P("chan", ("groups", "seq"), "section"))
    return jax.shard_map(
        per_device, mesh=mesh, in_specs=in_specs, out_specs=out_specs, check_vma=False
    )
```

profile of v0, /device:TPU:0, one launch (start us, length us, event | category | flops | bytes accessed | tf_op | source)
XLA Modules:
  0.0 73.6 jit_solution(9603304205572424095)
XLA Ops:
  0.6 0.0 copy-start
  0.7 1.0 %eq.22 = s32[512,16]{1,0:T(8,128)S(1)} reshape(s32[8192]{0:T(1024)} %param.10) | data formatting | bytes 65536 | tf_op jit(solution)/shard_map/eq | solution.py:79
  1.6 0.1 copy.16
  1.8 0.1 eq.26
  1.9 1.2 %convolution_convert_fusion = bf16[512,384]{1,0:T(8,128)(2,1)S(1)} fusion(s32[512,64]{0,1:T(8,128)S(1)} %eq.24, s32[64]{0:T(128)S(1)} %eq.26, bf16[64,768]{1,0:T(8,128)(2,1)} %param.11, s32[]{:T(128)S(6)} %select_n.16), kind=kOutput, calls=%fused_computation.7 | convolution fusion | flops 25395200 | bytes 573700 | tf_op jit(solution)/shard_map/dot_general | solution.py:86
  3.1 2.5 %all_gather.15 = bf16[512,768]{1,0:T(8,128)(2,1)S(1)} all-gather(bf16[512,384]{1,0:T(8,128)(2,1)S(1)} %convolution_convert_fusion), channel_id=1, replica_groups=mesh['groups'=2,'seq'=4,'section'=2,'chan'=2] {'chan'}, dimensions={1}, use_global_device_ids=true | all-gather | bytes 1179648 | tf_op jit(solution)/shard_map/all_gather | solution.py:87
  5.6 4.8 %collective-permute-start = (bf16[4,768]{1,0:T(4,128)(2,1)S(1)}, bf16[4,768]{1,0:T(4,128)(2,1)S(1)}, u32[]{:S(2)}, u32[]{:S(2)}) collective-permute-start(bf16[4,768]{1,0:T(4,128)(2,1)S(1)} %get-tuple-element.4), channel_id=1, source_target_pairs={{0,2},{2,4},{4,6},{6,8},{8,10},{10,12},{12,14},{1,3},{3,5},{5,7},{... | collective-permute-start | bytes 18440 | tf_op jit(solution)/shard_map/ppermute | solution.py:25
  10.3 1.3 %collective-permute-start.1 = (bf16[4,768]{1,0:T(4,128)(2,1)S(1)}, bf16[4,768]{1,0:T(4,128)(2,1)S(1)}, u32[]{:S(2)}, u32[]{:S(2)}) collective-permute-start(bf16[4,768]{1,0:T(4,128)(2,1)S(1)} %get-tuple-element.5), channel_id=1, source_target_pairs={{2,0},{4,2},{6,4},{8,6},{10,8},{12,10},{14,12},{3,1},{5,3},{7,5},{... | collective-permute-start | bytes 18440 | tf_op jit(solution)/shard_map/ppermute | solution.py:27
  11.7 0.1 log-plus-one_multiply_fusion
  11.8 0.1 broadcast_and_fusion
  11.9 0.0 collective-permute-done
  11.9 4.0 %collective-permute-done.1 = bf16[4,768]{1,0:T(4,128)(2,1)S(1)} collective-permute-done((bf16[4,768]{1,0:T(4,128)(2,1)S(1)}, bf16[4,768]{1,0:T(4,128)(2,1)S(1)}, u32[]{:S(2)}, u32[]{:S(2)}) %collective-permute-start.1) | collective-permute-done | bytes 6176 | tf_op jit(solution)/shard_map/ppermute | solution.py:27
  15.9 0.3 fusion
  16.2 0.0 copy-done.6
  16.2 0.3 fusion.2
  16.6 0.0 copy-done.2
  16.6 0.6 fusion.34
  17.1 0.6 convolution_add_fusion.1
  17.7 0.8 %fusion.24 = bf16[512,384]{1,0:T(8,128)(2,1)S(1)} fusion(f32[512,384]{1,0:T(8,128)S(1)} %convolution_add_fusion.1, bf16[520,768]{1,0:T(8,128)(2,1)S(1)} %fusion.2, bf16[512,384]{1,0:T(8,128)(2,1)S(1)} %convolution_convert_fusion, bf16[3,768,384]{2,1,0:T(8,128)(2,1)S(1)} %copy-done.2), kind=kOutput, calls=%fused_computation.43 | convolution fusion | flops 304349184 | bytes 2949120 | tf_op jit(solution)/shard_map/dot_general | solution.py:92
  18.5 0.6 slice.172
  19.1 0.6 slice.173
  19.7 0.1 max.3
  19.8 2.1 %all_gather.16 = bf16[256,768]{1,0:T(8,128)(2,1)S(1)} all-gather(bf16[256,384]{1,0:T(8,128)(2,1)S(1)} %max.3), channel_id=1, replica_groups=mesh['groups'=2,'seq'=4,'section'=2,'chan'=2] {'chan'}, dimensions={1}, use_global_device_ids=true | all-gather | bytes 589824 | tf_op jit(solution)/shard_map/all_gather | solution.py:102
  21.9 0.0 copy-done
  21.9 0.0 copy-start.3
  21.9 1.4 %convert_reduce_fusion = (f32[4,768]{1,0:T(4,128)S(1)}, bf16[256,768]{1,0:T(8,128)(2,1)}) fusion(bf16[256,768]{1,0:T(8,128)(2,1)S(1)} %all_gather.16, bf16[768,768]{1,0:T(8,128)(2,1)S(1)} %copy-done), kind=kOutput, calls=%fused_computation.56 | convolution fusion | flops 304149504 | bytes 1978368 | tf_op jit(solution)/shard_map/dot_general | solution.py:101
  23.3 1.8 %all_gather.17 = bf16[4,1536]{1,0:T(4,128)(2,1)S(1)} all-gather(bf16[4,768]{1,0:T(4,128)(2,1)S(1)} %multiply_convert_fusion), channel_id=1, replica_groups=mesh['groups'=2,'seq'=4,'section'=2,'chan'=2] {'chan'}, dimensions={1}, use_global_device_ids=true | all-gather | bytes 18432 | tf_op jit(solution)/shard_map/all_gather | solution.py:111
  25.1 0.1 fusion.87
  25.2 0.0 copy-done.1
  25.2 0.0 copy-done.5
  25.2 0.2 fusion.15
  25.5 26.5 %all-gather = bf16[8,4,256]{2,1,0:T(4,128)(2,1)S(1)} all-gather(bf16[1,4,256]{2,1,0:T(4,128)(2,1)S(1)} %fusion.15), channel_id=1, replica_groups=mesh['groups'=2,'seq'=4,'section'=2,'chan'=2] {'seq','section'}, dimensions={0}, use_global_device_ids=true | all-gather | bytes 18432 | tf_op jit(solution)/shard_map/all_gather | solution.py:124
  52.0 0.1 convert_bitcast_fusion
  52.1 0.1 add_convert_fusion
  52.3 0.0 copy-done.3
  52.3 0.1 fusion.85
  52.4 0.1 convolution_add_fusion.11
  52.5 0.1 convolution_add_fusion.10
  52.7 0.1 convolution_add_fusion.9
  52.8 0.1 convolution_add_fusion.8
  53.0 0.1 convolution_add_fusion.7
  53.1 0.1 convolution_add_fusion.6
  53.2 0.1 convolution_add_fusion.5
  53.4 0.1 fusion.13
  53.6 0.1 copy.17
  53.7 2.0 %all_gather.19 = bf16[128,8,16]{2,1,0:T(8,128)(2,1)S(1)} all-gather(bf16[64,8,16]{2,1,0:T(8,128)(2,1)S(1)} %copy.17), channel_id=1, replica_groups=mesh['groups'=2,'seq'=4,'section'=2,'chan'=2] {'chan'}, dimensions={0}, use_global_device_ids=true | all-gather | bytes 49152 | tf_op jit(solution)/shard_map/all_gather | solution.py:144
  55.7 0.2 copy.18
  55.9 2.1 %collective-permute-start.2 = (bf16[128,1,16]{0,2,1:T(8,128)(2,1)S(1)}, bf16[128,1,16]{0,2,1:T(8,128)(2,1)S(1)}, u32[]{:S(2)}, u32[]{:S(2)}) collective-permute-start(bf16[128,1,16]{0,2,1:T(8,128)(2,1)S(1)} %get-tuple-element.10), channel_id=1, source_target_pairs={{0,4},{4,8},{8,12},{1,5},{5,9},{9,13},{2,6},{6,10},{10,14},{3,7},{... | collective-permute-start | bytes 12296 | tf_op jit(solution)/shard_map/ppermute | solution.py:25
  58.1 1.3 %collective-permute-start.3 = (bf16[128,1,16]{0,2,1:T(8,128)(2,1)S(1)}, bf16[128,1,16]{0,2,1:T(8,128)(2,1)S(1)}, u32[]{:S(2)}, u32[]{:S(2)}) collective-permute-start(bf16[128,1,16]{0,2,1:T(8,128)(2,1)S(1)} %get-tuple-element.11), channel_id=1, source_target_pairs={{4,0},{8,4},{12,8},{5,1},{9,5},{13,9},{6,2},{10,6},{14,10},{7,3},{... | collective-permute-start | bytes 12296 | tf_op jit(solution)/shard_map/ppermute | solution.py:27
  59.4 0.1 fusion.94
  59.5 0.0 collective-permute-done.2
  59.5 4.0 %collective-permute-done.3 = bf16[128,1,16]{0,2,1:T(8,128)(2,1)S(1)} collective-permute-done((bf16[128,1,16]{0,2,1:T(8,128)(2,1)S(1)}, bf16[128,1,16]{0,2,1:T(8,128)(2,1)S(1)}, u32[]{:S(2)}, u32[]{:S(2)}) %collective-permute-start.3) | collective-permute-done | bytes 4128 | tf_op jit(solution)/shard_map/ppermute | solution.py:27
  63.6 3.0 %collective-permute-start.4 = (bf16[128,10,1]{0,2,1:T(2,128)(2,1)S(1)}, bf16[128,10,1]{0,2,1:T(2,128)(2,1)S(1)}, u32[]{:S(2)}, u32[]{:S(2)}) collective-permute-start(bf16[128,10,1]{0,2,1:T(2,128)(2,1)S(1)} %get-tuple-element.8), channel_id=1, source_target_pairs={{0,2},{1,3},{4,6},{5,7},{8,10},{9,11},{12,14},{13,15},{16,18},{17,... | collective-permute-start | bytes 7688 | tf_op jit(solution)/shard_map/ppermute | solution.py:25
  66.6 1.3 %collective-permute-start.5 = (bf16[128,10,1]{0,2,1:T(2,128)(2,1)S(1)}, bf16[128,10,1]{0,2,1:T(2,128)(2,1)S(1)}, u32[]{:S(2)}, u32[]{:S(2)}) collective-permute-start(bf16[128,10,1]{0,2,1:T(2,128)(2,1)S(1)} %get-tuple-element.9), channel_id=1, source_target_pairs={{2,0},{3,1},{6,4},{7,5},{10,8},{11,9},{14,12},{15,13},{18,16},{19,... | collective-permute-start | bytes 7688 | tf_op jit(solution)/shard_map/ppermute | solution.py:27
  67.9 0.1 fusion.59
  68.0 0.1 fusion.63
  68.2 0.0 collective-permute-done.4
  68.2 4.0 %collective-permute-done.5 = bf16[128,10,1]{0,2,1:T(2,128)(2,1)S(1)} collective-permute-done((bf16[128,10,1]{0,2,1:T(2,128)(2,1)S(1)}, bf16[128,10,1]{0,2,1:T(2,128)(2,1)S(1)}, u32[]{:S(2)}, u32[]{:S(2)}) %collective-permute-start.5) | collective-permute-done | bytes 2592 | tf_op jit(solution)/shard_map/ppermute | solution.py:27
  72.2 0.1 fusion.74
  72.3 0.1 fusion.67
  72.4 0.1 fusion.72
  72.6 0.1 fusion.69
  72.7 0.2 fusion.9
  72.9 0.8 %fusion.14 = bf16[64,8,16]{0,2,1:T(8,128)(2,1)} fusion(f32[8,16,64]{2,1,0:T(8,128)S(1)} %fusion.67, f32[8,16,64]{2,1,0:T(8,128)S(1)} %fusion.63, f32[8,16,64]{2,1,0:T(8,128)S(1)} %fusion.69, f32[8,16,64]{2,1,0:T(8,128)S(1)} %fusion.9, bf16[64,8,16]{0,2,1:T(8,128)(2,1)S(1)} %fusion.13, bf16[128,10,17]{0,2,1:T(8,128)(2,1)S(1)} %get-tuple-element.7, ...), kind=kOutput, calls=%fused_computation.31 | convolution fusion | flops 2154496 | bytes 360448 | tf_op jit(solution)/shard_map/co,crs->ors/dot_general | solution.py:46
  (26 shorter events, 0.3 us)
Async XLA Ops:
  0.6 21.3 %copy-start = (bf16[768,768]{1,0:T(8,128)(2,1)S(1)}, bf16[768,768]{1,0:T(8,128)(2,1)}, u32[]{:S(2)}) copy-start(bf16[768,768]{1,0:T(8,128)(2,1)} %param.14) | copy-start | bytes 3538948
  1.7 14.5 %copy-start.6 = (f32[768]{0:T(1024)S(1)}, f32[768]{0:T(1024)}, u32[]{:S(2)}) copy-start(f32[768]{0:T(1024)} %param.12) | copy-start | bytes 9220
  5.6 6.3 %collective-permute-start = (bf16[4,768]{1,0:T(4,128)(2,1)S(1)}, bf16[4,768]{1,0:T(4,128)(2,1)S(1)}, u32[]{:S(2)}, u32[]{:S(2)}) collective-permute-start(bf16[4,768]{1,0:T(4,128)(2,1)S(1)} %get-tuple-element.4), channel_id=1, source_target_pairs={{0,2},{2,4},{4,6},{6,8},{8,10},{10,12},{12,14},{1,3},{3,5},{5,7},{... | collective-permute-start | bytes 18440 | tf_op jit(solution)/shard_map/ppermute | solution.py:25
  10.3 5.5 %collective-permute-start.1 = (bf16[4,768]{1,0:T(4,128)(2,1)S(1)}, bf16[4,768]{1,0:T(4,128)(2,1)S(1)}, u32[]{:S(2)}, u32[]{:S(2)}) collective-permute-start(bf16[4,768]{1,0:T(4,128)(2,1)S(1)} %get-tuple-element.5), channel_id=1, source_target_pairs={{2,0},{4,2},{6,4},{8,6},{10,8},{12,10},{14,12},{3,1},{5,3},{7,5},{... | collective-permute-start | bytes 18440 | tf_op jit(solution)/shard_map/ppermute | solution.py:27
  11.9 4.7 %copy-start.2 = (bf16[3,768,384]{2,1,0:T(8,128)(2,1)S(1)}, bf16[3,768,384]{2,1,0:T(8,128)(2,1)}, u32[]{:S(2)}) copy-start(bf16[3,768,384]{2,1,0:T(8,128)(2,1)} %param.13) | copy-start | bytes 5308420
  21.9 3.3 %copy-start.1 = (bf16[1536,256]{1,0:T(8,128)(2,1)S(1)}, bf16[1536,256]{1,0:T(8,128)(2,1)}, u32[]{:S(2)}) copy-start(bf16[1536,256]{1,0:T(8,128)(2,1)} %param.16) | copy-start | bytes 2359300
  21.9 3.3 %copy-start.5 = (f32[1536]{0:T(1024)S(1)}, f32[1536]{0:T(1024)}, u32[]{:S(2)}) copy-start(f32[1536]{0:T(1024)} %param.15) | copy-start | bytes 18436
  21.9 30.2 %copy-start.7 = (f32[128]{0:T(128)S(1)}, f32[128]{0:T(128)}, u32[]{:S(2)}) copy-start(f32[128]{0:T(128)} %param.17) | copy-start | bytes 1540
  21.9 30.4 %copy-start.3 = (bf16[3,3,128,64]{2,3,1,0:T(8,128)(2,1)S(1)}, bf16[3,3,128,64]{2,3,1,0:T(8,128)(2,1)}, u32[]{:S(2)}) copy-start(bf16[3,3,128,64]{2,3,1,0:T(8,128)(2,1)} %param.18) | copy-start | bytes 442372
  25.5 33.9 %copy-start.4 = (bf16[3,3,128,64]{2,3,1,0:T(8,128)(2,1)S(1)}, bf16[3,3,128,64]{2,3,1,0:T(8,128)(2,1)}, u32[]{:S(2)}) copy-start(bf16[3,3,128,64]{2,3,1,0:T(8,128)(2,1)} %param.19) | copy-start | bytes 442372
  55.9 3.6 %collective-permute-start.2 = (bf16[128,1,16]{0,2,1:T(8,128)(2,1)S(1)}, bf16[128,1,16]{0,2,1:T(8,128)(2,1)S(1)}, u32[]{:S(2)}, u32[]{:S(2)}) collective-permute-start(bf16[128,1,16]{0,2,1:T(8,128)(2,1)S(1)} %get-tuple-element.10), channel_id=1, source_target_pairs={{0,4},{4,8},{8,12},{1,5},{5,9},{9,13},{2,6},{6,10},{10,14},{3,7},{... | collective-permute-start | bytes 12296 | tf_op jit(solution)/shard_map/ppermute | solution.py:25
  58.1 5.5 %collective-permute-start.3 = (bf16[128,1,16]{0,2,1:T(8,128)(2,1)S(1)}, bf16[128,1,16]{0,2,1:T(8,128)(2,1)S(1)}, u32[]{:S(2)}, u32[]{:S(2)}) collective-permute-start(bf16[128,1,16]{0,2,1:T(8,128)(2,1)S(1)} %get-tuple-element.11), channel_id=1, source_target_pairs={{4,0},{8,4},{12,8},{5,1},{9,5},{13,9},{6,2},{10,6},{14,10},{7,3},{... | collective-permute-start | bytes 12296 | tf_op jit(solution)/shard_map/ppermute | solution.py:27
  63.6 4.6 %collective-permute-start.4 = (bf16[128,10,1]{0,2,1:T(2,128)(2,1)S(1)}, bf16[128,10,1]{0,2,1:T(2,128)(2,1)S(1)}, u32[]{:S(2)}, u32[]{:S(2)}) collective-permute-start(bf16[128,10,1]{0,2,1:T(2,128)(2,1)S(1)} %get-tuple-element.8), channel_id=1, source_target_pairs={{0,2},{1,3},{4,6},{5,7},{8,10},{9,11},{12,14},{13,15},{16,18},{17,... | collective-permute-start | bytes 7688 | tf_op jit(solution)/shard_map/ppermute | solution.py:25
  66.6 5.5 %collective-permute-start.5 = (bf16[128,10,1]{0,2,1:T(2,128)(2,1)S(1)}, bf16[128,10,1]{0,2,1:T(2,128)(2,1)S(1)}, u32[]{:S(2)}, u32[]{:S(2)}) collective-permute-start(bf16[128,10,1]{0,2,1:T(2,128)(2,1)S(1)} %get-tuple-element.9), channel_id=1, source_target_pairs={{2,0},{3,1},{6,4},{7,5},{10,8},{11,9},{14,12},{15,13},{18,16},{19,... | collective-permute-start | bytes 7688 | tf_op jit(solution)/shard_map/ppermute | solution.py:27
where the time goes:
time: 74 us; the launch traced here: 73.6 us
  blocking collectives  34.8 us (47%)
  starting transfers between devices  13.8 us (19%)
  waiting for transfers between devices  12 us (16%)
  matrix products  7.84 us (11%)
  local copies, waits for them, and re-layouts  2.83 us (4%)
  other arithmetic  1.39 us (2%)
  between operations  0.97 us (1%)
    all_gather x1, blocking collectives, per_device(): lax.all_gather(factors, ('seq', 'section'), axis=0, tiled=True)  26.5 us
    ppermute x3, waiting for transfers between devices, padded(): lax.ppermute(head, axis, [((i + 1) % count, i) for i in range(ends)])  12 us
    ppermute x3, starting transfers between devices, padded(): lax.ppermute(tail, axis, [(i, (i + 1) % count) for i in range(ends)])  9.91 us
    ppermute x3, starting transfers between devices, padded(): lax.ppermute(head, axis, [((i + 1) % count, i) for i in range(ends)])  3.88 us
    dot_general x18, matrix products, pair_conv(): jnp.einsum('co,crs->ors', weight[shift_row, shift_col], window, preferred...  3.11 us
    all_gather x1, blocking collectives, per_device(): full_stem_output = lax.all_gather(stem_own, 'chan', axis=1, tiled=True)  2.45 us
    all_gather x1, blocking collectives, per_device(): lax.all_gather(halved, 'chan', axis=1, tiled=True)  2.09 us
    all_gather x1, blocking collectives, per_device(): mid_full = lax.all_gather(pair_mid, 'chan', axis=0, tiled=True)  1.99 us
  transfers between devices with their start and end apart: 6, of which 3 were waited for; matrix products, arithmetic and copies ran while one was open for 1% of the time, Pallas kernels for 0%

commit v1 on v0

v1 whole, which is shorter than its diff:
```python
import functools
import math

import jax
import jax.numpy as jnp
from jax import lax
from jax.experimental import pallas as pl
from jax.experimental.pallas import tpu as pltpu
from jax.sharding import PartitionSpec as P

PATCH = 16
POOL = 64
DILATION_ROWS = 4
CHUNKS = 2
MESH = pl.DeviceIdType.MESH
epsilon = 1e-06
f32 = jnp.float32
bf16 = jnp.bfloat16


def round_up(value, unit):
    return -(-value // unit) * unit


def iota(shape, dim):
    return lax.broadcasted_iota(jnp.int32, shape, dim)


def rounded(value):
    return value.astype(bf16).astype(f32)


def dot(a, b):
    return jnp.dot(a, b, preferred_element_type=f32)


def kernel(
    n_seq,
    n_sec,
    codes,
    stem_weight,
    conv_gain,
    dilated_weight,
    widen_weight,
    token_gain,
    proj_weight,
    dist_weight,
    pair_one,
    pair_two,
    fine_out,
    pair_out,
    codes_ext,
    stem_w,
    gain_w,
    dil_w,
    wid_w,
    tgain_w,
    proj_w,
    dist_w,
    one_w,
    two_w,
    stem_scr,
    norm_scr,
    halved,
    fine,
    tokens,
    factors,
    row_fac,
    col_fac,
    dist_scr,
    start_scr,
    act_scr,
    mid_scr,
    act_two_scr,
    load_sem,
    halo_send,
    halo_recv,
    one_send,
    one_recv,
    half_send,
    half_recv,
    tok_send,
    tok_recv,
    fac_send,
    fac_recv,
    out_sem,
):
    count = n_seq * n_sec
    seq, section, chan = lax.axis_index("seq"), lax.axis_index("section"), lax.axis_index("chan")
    pos = seq * n_sec + section
    other = 1 - chan
    code_rows = codes.shape[0]
    half_rows = halved.shape[1]
    rows = 2 * half_rows
    own_width = halved.shape[2]
    tok_count = half_rows // POOL
    total = tok_count * count
    tile_h, tile_w = tok_count * n_sec, tok_count * n_seq
    start_h, start_w = start_scr.shape[0], start_scr.shape[1]
    mid_h, mid_w = mid_scr.shape[0], mid_scr.shape[1]
    pc = start_scr.shape[2]

    def place(index):
        return {"seq": index // n_sec, "section": index % n_sec}

    def each_peer(body):
        if count <= 16:
            for d in range(1, count):
                body(d)
        else:
            lax.fori_loop(1, count, lambda d, c: (body(d), c)[1], 0)

    pairs = [
        (codes, codes_ext.at[pl.ds(8, code_rows)]),
        (stem_weight, stem_w),
        (conv_gain, gain_w),
        (dilated_weight, dil_w),
        (widen_weight, wid_w),
        (token_gain, tgain_w),
        (proj_weight, proj_w),
        (dist_weight, dist_w),
        (pair_one, one_w.at[chan]),
        (pair_two, two_w),
    ]
    loads = [pltpu.make_async_copy(a, b, load_sem.at[i]) for i, (a, b) in enumerate(pairs)]
    l_codes, l_stem, l_gain, l_dil, l_wid, l_tgain, l_proj, l_dist, l_one, l_two = loads
    for load in loads:
        load.start()

    barrier = pltpu.get_barrier_semaphore()
    pl.semaphore_signal(barrier, inc=1, device_id={"chan": other}, device_id_type=MESH)

    def greet(d):
        peer = lax.rem(pos + d, count)
        pl.semaphore_signal(barrier, inc=1, device_id=place(peer), device_id_type=MESH)

    each_peer(greet)
    pl.semaphore_wait(barrier, count)

    to_next = pltpu.make_async_remote_copy(
        src_ref=codes.at[pl.ds(code_rows - 8, 8)],
        dst_ref=codes_ext.at[pl.ds(0, 8)],
        send_sem=halo_send.at[0],
        recv_sem=halo_recv.at[0],
        device_id=place(lax.rem(pos + 1, count)),
        device_id_type=MESH,
    )
    to_prev = pltpu.make_async_remote_copy(
        src_ref=codes.at[pl.ds(0, 8)],
        dst_ref=codes_ext.at[pl.ds(8 + code_rows, 8)],
        send_sem=halo_send.at[1],
        recv_sem=halo_recv.at[1],
        device_id=place(lax.rem(pos + count - 1, count)),
        device_id_type=MESH,
    )
    one_copy = pltpu.make_async_remote_copy(
        src_ref=pair_one,
        dst_ref=one_w.at[chan],
        send_sem=one_send,
        recv_sem=one_recv,
        device_id={"chan": other},
        device_id_type=MESH,
    )
    one_in = pltpu.make_async_remote_copy(
        src_ref=pair_one,
        dst_ref=one_w.at[other],
        send_sem=one_send,
        recv_sem=one_recv,
        device_id={"chan": other},
        device_id_type=MESH,
    )
    first, last = pos == 0, pos == count - 1

    @pl.when(jnp.logical_not(last))
    def _():
        to_next.start()

    @pl.when(jnp.logical_not(first))
    def _():
        to_prev.start()

    one_copy.start()

    row_anchor, col_anchor = seq * tile_h, section * tile_w
    row_fac[...] = jnp.zeros_like(row_fac)
    col_fac[...] = jnp.zeros_like(col_fac)
    l_dist.wait()
    weight = dist_w[...]
    col_index = col_anchor - 2 + iota((start_w, pc), 0)
    for i in range(start_h):
        gap = jnp.abs(col_index - (row_anchor - 2 + i)).astype(f32)
        dist_scr[i] = jnp.log1p(gap) / math.log(total) * weight

    @pl.when(first)
    def _():
        codes_ext[pl.ds(0, 8), :] = jnp.zeros((8, codes_ext.shape[1]), jnp.int32)

    @pl.when(jnp.logical_not(first))
    def _():
        to_next.wait_recv()

    @pl.when(last)
    def _():
        codes_ext[pl.ds(8 + code_rows, 8), :] = jnp.zeros((8, codes_ext.shape[1]), jnp.int32)

    @pl.when(jnp.logical_not(last))
    def _():
        to_prev.wait_recv()

    l_codes.wait()
    reach = DILATION_ROWS // 2
    ext = norm_scr.shape[0] // 2
    per_row = codes_ext.shape[1] // PATCH
    shift = 8 * per_row

    def patch_of(shape):
        line = iota(shape, 0)
        odd = (line >= ext).astype(jnp.int32)
        return 2 * (line - ext * odd - reach) + odd

    ext_rows = codes_ext.shape[0]
    lanes = codes_ext.shape[1]
    taken = ((patch_of((2 * ext, ext_rows)) + shift) // per_row) == iota((2 * ext, ext_rows), 1)
    spread = dot(taken.astype(f32).astype(bf16), codes_ext[...].astype(f32).astype(bf16))
    patch = patch_of((2 * ext, lanes))
    mine = (iota((2 * ext, lanes), 1) // PATCH) == ((patch + shift) % per_row)
    spread = jnp.where(mine, spread, 0.0).astype(bf16)
    select = (iota((lanes, 4 * PATCH), 0) % PATCH) == (iota((lanes, 4 * PATCH), 1) // 4)
    code = dot(spread, select.astype(f32).astype(bf16))
    patch = patch_of((2 * ext, 4 * PATCH))
    low = jnp.where(first, 0, -shift)
    high = jnp.where(last, rows, rows + shift)
    letter = (iota((2 * ext, 4 * PATCH), 1) % 4).astype(f32)
    hit = (code == letter) & (patch >= low) & (patch < high)
    onehot = jnp.where(hit, 1.0, 0.0).astype(bf16)

    l_stem.wait()
    l_gain.wait()
    square = jnp.zeros((2 * ext, 1), f32)
    stems = []
    for part in range(2):
        stem = rounded(dot(onehot, stem_w[:, part * own_width : (part + 1) * own_width]))
        stem_scr[part] = stem
        stems.append(stem)
        square = square + jnp.sum(stem * stem, axis=1, keepdims=True)
    scale = lax.rsqrt(square / (2 * own_width) + epsilon)
    for part in range(2):
        cols = slice(part * own_width, (part + 1) * own_width)
        norm_scr[:, cols] = stems[part] * scale * gain_w[:, cols]

    l_dil.wait()
    piece = half_rows // CHUNKS
    half_copies = []
    for c in range(CHUNKS):
        taps = None
        for k in range(3):
            at = c * piece + k * reach
            window = jnp.concatenate(
                [norm_scr[at : at + piece, :], norm_scr[ext + at : ext + at + piece, :]], axis=0
            ).astype(bf16)
            term = dot(window, dil_w[k])
            taps = term if taps is None else taps + term
        at = c * piece + reach
        stem_own = jnp.concatenate(
            [stem_scr[chan, at : at + piece, :], stem_scr[chan, ext + at : ext + at + piece, :]], axis=0
        )
        tower = stem_own + jax.nn.gelu(taps)
        top = jnp.maximum(tower[:piece], tower[piece:]).astype(bf16)
        span = pl.ds(c * piece, piece)
        halved[chan, span, :] = top
        copy = pltpu.make_async_remote_copy(
            src_ref=halved.at[chan, span],
            dst_ref=halved.at[chan, span],
            send_sem=half_send.at[c],
            recv_sem=half_recv.at[c],
            device_id={"chan": other},
            device_id_type=MESH,
        )
        copy.start()
        half_copies.append(copy)

    l_wid.wait()
    pieces = []
    for c in range(CHUNKS):
        span = pl.ds(c * piece, piece)
        own_k = pl.ds(pl.multiple_of(chan * own_width, own_width), own_width)
        other_k = pl.ds(pl.multiple_of(other * own_width, own_width), own_width)
        wide = dot(halved[chan, span, :], wid_w[own_k, :])
        arrival = pltpu.make_async_remote_copy(
            src_ref=halved.at[chan, span],
            dst_ref=halved.at[other, span],
            send_sem=half_send.at[c],
            recv_sem=half_recv.at[c],
            device_id={"chan": other},
            device_id_type=MESH,
        )
        arrival.wait_recv()
        wide = wide + dot(halved[other, span, :], wid_w[other_k, :])
        feature = jax.nn.gelu(wide).astype(bf16)
        fine[span, :] = feature
        feature = feature.astype(f32)
        for t in range(piece // POOL):
            mean = jnp.sum(feature[t * POOL : (t + 1) * POOL], axis=0, keepdims=True) * (1.0 / POOL)
            pieces.append(rounded(mean))
    out_copy = pltpu.make_async_copy(fine, fine_out, out_sem)
    out_copy.start()
    for t in range(tokens.shape[1]):
        value = pieces[t] if t < tok_count else jnp.zeros_like(pieces[0])
        tokens[chan, t : t + 1, :] = value
    tok_copy = pltpu.make_async_remote_copy(
        src_ref=tokens.at[chan],
        dst_ref=tokens.at[chan],
        send_sem=tok_send,
        recv_sem=tok_recv,
        device_id={"chan": other},
        device_id_type=MESH,
    )
    tok_copy.start()
    l_tgain.wait()
    l_proj.wait()
    tok_in = pltpu.make_async_remote_copy(
        src_ref=tokens.at[chan],
        dst_ref=tokens.at[other],
        send_sem=tok_send,
        recv_sem=tok_recv,
        device_id={"chan": other},
        device_id_type=MESH,
    )
    tok_in.wait_recv()
    whole = jnp.concatenate([tokens[0], tokens[1]], axis=1)
    mean_square = jnp.sum(whole * whole, axis=1, keepdims=True) / whole.shape[1]
    token_norm = (whole * lax.rsqrt(mean_square + epsilon) * tgain_w[...]).astype(bf16)
    factor = rounded(dot(token_norm, proj_w[...]))
    factors[pos, 0:tok_count, :] = factor[:tok_count, :pc]
    factors[pos, tok_count : 2 * tok_count, :] = factor[:tok_count, pc:]

    def send_factor(d):
        peer = lax.rem(pos + d, count)
        pltpu.make_async_remote_copy(
            src_ref=factors.at[pos],
            dst_ref=factors.at[pos],
            send_sem=fac_send.at[d],
            recv_sem=fac_recv.at[pos],
            device_id=place(peer),
            device_id_type=MESH,
        ).start()

    each_peer(send_factor)

    def take_factor(d):
        source = lax.rem(pos + count - d, count)
        pltpu.make_async_remote_copy(
            src_ref=factors.at[pos],
            dst_ref=factors.at[source],
            send_sem=fac_send.at[d],
            recv_sem=fac_recv.at[source],
            device_id=place(source),
            device_id_type=MESH,
        ).wait_recv()

    each_peer(take_factor)
    for s in range(count):
        at = 8 + s * tok_count
        row_fac[at : at + tok_count, :] = factors[s, 0:tok_count, :]
        col_fac[at : at + tok_count, :] = factors[s, tok_count : 2 * tok_count, :]

    near = col_fac[pl.ds(pl.multiple_of(col_anchor, 8), start_w + 8), :][6 : 6 + start_w]
    col_in = (col_index >= 0) & (col_index < total)
    for i in range(start_h):
        row_here = row_fac[pl.ds(row_anchor + 6 + i, 1), :]
        begin = rounded(row_here * near + dist_scr[i])
        start_scr[i] = begin
        row_index = jnp.zeros_like(col_index) + (row_anchor - 2 + i)
        inside = col_in & (row_index >= 0) & (row_index < total)
        act_scr[i] = jnp.where(inside, jax.nn.gelu(begin), 0.0)

    one_in.wait_recv()
    l_one.wait()
    windows = [
        act_scr[a : a + mid_h, b : b + mid_w, :].reshape(mid_h * mid_w, pc).astype(bf16)
        for a in range(3)
        for b in range(3)
    ]
    flat = jnp.concatenate(windows, axis=1)
    conv = jnp.concatenate([dot(flat, one_w[0]), dot(flat, one_w[1])], axis=1)
    middle = rounded(start_scr[1 : 1 + mid_h, 1 : 1 + mid_w, :].reshape(mid_h * mid_w, pc) + conv)
    mid_scr[...] = middle.reshape(mid_h, mid_w, pc)
    col_mid = col_anchor - 1 + iota((mid_w, pc), 0)
    col_in = (col_mid >= 0) & (col_mid < total)
    for i in range(mid_h):
        row_index = jnp.zeros_like(col_mid) + (row_anchor - 1 + i)
        inside = col_in & (row_index >= 0) & (row_index < total)
        act_two_scr[i] = jnp.where(inside, jax.nn.gelu(mid_scr[i]), 0.0)

    l_two.wait()
    windows = [
        act_two_scr[a : a + tile_h, b : b + tile_w, :].reshape(tile_h * tile_w, pc).astype(bf16)
        for a in range(3)
        for b in range(3)
    ]
    conv = dot(jnp.concatenate(windows, axis=1), two_w[...])
    middle = mid_scr[1 : 1 + tile_h, 1 : 1 + tile_w, :].reshape(tile_h * tile_w, pc)
    width = conv.shape[1]
    own = jnp.where(chan == 0, middle[:, :width], middle[:, width:])
    pair_out[...] = (own + conv).astype(pair_out.dtype)

    @pl.when(jnp.logical_not(last))
    def _():
        to_next.wait_send()

    @pl.when(jnp.logical_not(first))
    def _():
        to_prev.wait_send()

    one_copy.wait_send()
    for copy in half_copies:
        copy.wait_send()
    tok_copy.wait_send()

    def sent(d):
        pltpu.make_async_remote_copy(
            src_ref=factors.at[pos],
            dst_ref=factors.at[pos],
            send_sem=fac_send.at[d],
            recv_sem=fac_recv.at[pos],
            device_id=place(lax.rem(pos + d, count)),
            device_id_type=MESH,
        ).wait_send()

    each_peer(sent)
    out_copy.wait()


def per_device(
    n_seq,
    n_sec,
    base_codes,
    stem_weight,
    conv_gain,
    dilated_conv_weight,
    widen_weight,
    token_gain,
    proj_weight,
    dist_weight,
    pair_weight_one,
    pair_weight_two,
):
    lanes = 128
    count = n_seq * n_sec
    codes = base_codes.reshape(-1, lanes)
    half_rows = base_codes.shape[0] // PATCH // 2
    channels = stem_weight.shape[1]
    own_width = dilated_conv_weight.shape[2]
    wide = widen_weight.shape[1]
    pc, pc_own = pair_weight_one.shape[2], pair_weight_one.shape[3]
    tok_count = half_rows // POOL
    tile_h, tile_w = tok_count * n_sec, tok_count * n_seq
    mid_h, mid_w = tile_h + 2, round_up(tile_w + 2, 8)
    start_h, start_w = tile_h + 4, round_up(mid_w + 2, 8)
    ext = round_up(half_rows + DILATION_ROWS, 8)
    total = tok_count * count
    one = pair_weight_one.reshape(-1, pc_own)
    two = pair_weight_two.reshape(-1, pc_own)
    gain, tgain, dist = conv_gain[None], token_gain[None], dist_weight[None]
    dma = pltpu.SemaphoreType.DMA
    anywhere = pl.BlockSpec(memory_space=pl.ANY)
    vmem = pltpu.VMEM
    fine, pair = pl.pallas_call(
        functools.partial(kernel, n_seq, n_sec),
        out_shape=(
            jax.ShapeDtypeStruct((half_rows, wide), bf16),
            jax.ShapeDtypeStruct((tile_h * tile_w, pc_own), f32),
        ),
        in_specs=[anywhere] * 10,
        out_specs=(anywhere, pl.BlockSpec(memory_space=pltpu.VMEM)),
        scratch_shapes=[
            vmem((codes.shape[0] + 16, lanes), jnp.int32),
            vmem(stem_weight.shape, bf16),
            vmem(gain.shape, f32),
            vmem(dilated_conv_weight.shape, bf16),
            vmem(widen_weight.shape, bf16),
            vmem(tgain.shape, f32),
            vmem(proj_weight.shape, bf16),
            vmem(dist.shape, f32),
            vmem((2,) + one.shape, bf16),
            vmem(two.shape, bf16),
            vmem((2, 2 * ext, own_width), f32),
            vmem((2 * ext, channels), f32),
            vmem((2, half_rows, own_width), bf16),
            vmem((half_rows, wide), bf16),
            vmem((2, round_up(tok_count, 8), wide), f32),
            vmem((count, 2 * tok_count, pc), f32),
            vmem((total + start_h + 16, pc), f32),
            vmem((total + start_w + 16, pc), f32),
            vmem((start_h, start_w, pc), f32),
            vmem((start_h, start_w, pc), f32),
            vmem((start_h, start_w, pc), f32),
            vmem((mid_h, mid_w, pc), f32),
            vmem((mid_h, mid_w, pc), f32),
            dma((10,)),
            dma((2,)),
            dma((2,)),
            dma,
            dma,
            dma((CHUNKS,)),
            dma((CHUNKS,)),
            dma,
            dma,
            dma((count,)),
            dma((count,)),
            dma,
        ],
        compiler_params=pltpu.CompilerParams(
            collective_id=0, has_side_effects=True, vmem_limit_bytes=48 * 1024 * 1024
        ),
    )(
        codes,
        stem_weight,
        gain,
        dilated_conv_weight,
        widen_weight,
        tgain,
        proj_weight,
        dist,
        one,
        two,
    )
    pair_map = pair.astype(bf16).T.reshape(pc_own, tile_h, tile_w)
    return fine, pair_map


def solution(mesh):
    in_specs = (
        P(("groups", "seq", "section")),
        P(),
        P(),
        P(None, None, "chan"),
        P(None, "chan"),
        P(),
        P(),
        P(),
        P(None, None, None, "chan"),
        P(None, None, None, "chan"),
    )
    out_specs = (P(("groups", "seq", "section"), "chan"), P("chan", ("groups", "seq"), "section"))
    body = functools.partial(per_device, mesh.shape["seq"], mesh.shape["section"])
    return jax.shard_map(
        body, mesh=mesh, in_specs=in_specs, out_specs=out_specs, check_vma=False
    )
```

time: 74 us -> 31.9 us (0.43)
  blocking collectives: 34.8 us -> 0 us
  Pallas kernels: 0 us -> 19.6 us
  starting transfers between devices: 13.8 us -> 0 us
  waiting for transfers between devices: 12 us -> 0 us
  matrix products: 7.84 us -> 0 us
  local copies, waits for them, and re-layouts: 2.83 us -> 10.6 us
  other arithmetic: 1.39 us -> 0.62 us
    all_gather x5 -> x0, blocking collectives: 34.8 us -> none  [the longest x1 26.5 us: per_device(): lax.all_gather(factors, ('seq', 'section'), axis=0, tiled=True)]
    pallas_call x0 -> x1, Pallas kernels: none -> 19.6 us  [per_device(): pl.pallas_call(functools.partial(kernel, n_seq, n_sec), out_shape=(jax.Sh...]
    ppermute x6 -> x0, starting transfers between devices: 13.8 us -> none  [the longest x3 9.91 us: padded(): lax.ppermute(tail, axis, [(i, (i + 1) % count) for i in range(ends)])]
    ppermute x6 -> x0, waiting for transfers between devices: 12 us -> none  [the longest x3 12 us: padded(): lax.ppermute(head, axis, [((i + 1) % count, i) for i in range(ends)])]
    unnamed x17 -> x15, local copies, waits for them, and re-layouts: 0.05 us -> 9.19 us
    dot_general x24 -> x0, matrix products: 7.84 us -> none  [the longest x18 3.11 us: pair_conv(): jnp.einsum('co,crs->ors', weight[shift_row, shift_col], window, preferred...]
    broadcast_in_dim x0 -> x2, local copies, waits for them, and re-layouts: none -> 1.39 us  [per_device(): gain, tgain, dist = (conv_gain[None], token_gain[None], dist_weight[None])]
    eq x6 -> x0, local copies, waits for them, and re-layouts: 1.23 us -> none  [per_device(): coded[:, :, None] == jnp.arange(4, dtype=jnp.int32)[None, None, :]]
  transfers between devices with their start and end apart: 6 -> 0, of which waited for: 3 -> 0; matrix products, arithmetic and copies ran while one was open for 1% -> 0% of each run, Pallas kernels for 0% -> 0%
where the time goes in v1:
time: 31.9 us; the launch traced here: 31.5 us
  Pallas kernels  19.6 us (61%)
  local copies, waits for them, and re-layouts  10.6 us (33%)
  between operations  0.65 us (2%)
  other arithmetic  0.62 us (2%)
    pallas_call x1, Pallas kernels, per_device(): pl.pallas_call(functools.partial(kernel, n_seq, n_sec), out_shape=(jax.Sh...  19.6 us
    unnamed x15, local copies, waits for them, and re-layouts  9.19 us
    broadcast_in_dim x2, local copies, waits for them, and re-layouts, per_device(): gain, tgain, dist = (conv_gain[None], token_gain[None], dist_weight[None])  1.39 us

profile of v1, /device:TPU:0, one launch (start us, length us, event | category | flops | bytes accessed | tf_op | source)
XLA Modules:
  0.0 31.5 jit_solution(9595455961769579078)
XLA Ops:
  0.6 0.7 %broadcast_in_dim.9.conv_gain = f32[1,768]{1,0:T(1,128)S(1)} reshape(f32[768]{0:T(1024)} %param.12) | data formatting | bytes 6144 | tf_op jit(solution)/shard_map/broadcast_in_dim | solution.py:464
  1.3 0.7 %broadcast_in_dim.10.token_gain = f32[1,1536]{1,0:T(1,128)S(1)} reshape(f32[1536]{0:T(1024)} %param.15) | data formatting | bytes 12288 | tf_op jit(solution)/shard_map/broadcast_in_dim | solution.py:464
  2.0 1.1 %copy.12 = bf16[3,3,128,64]{3,2,1,0:T(8,128)(2,1)S(1)} copy(bf16[3,3,128,64]{2,3,1,0:T(8,128)(2,1)} %param.18) | data formatting | bytes 294912 | tf_op args[8]
  3.1 1.1 %copy.13 = bf16[3,3,128,64]{3,2,1,0:T(8,128)(2,1)S(1)} copy(bf16[3,3,128,64]{2,3,1,0:T(8,128)(2,1)} %param.19) | data formatting | bytes 294912 | tf_op args[9]
  4.3 0.0 copy-start
  4.3 1.5 %copy-done = bf16[3,768,384]{2,1,0:T(8,128)(2,1)S(1)} copy-done((bf16[3,768,384]{2,1,0:T(8,128)(2,1)S(1)}, bf16[3,768,384]{2,1,0:T(8,128)(2,1)}, u32[]{:S(2)}) %copy-start) | copy-done | bytes 1769496
  5.8 0.0 copy-start.1
  5.8 1.3 %copy-done.1 = bf16[768,768]{1,0:T(8,128)(2,1)S(1)} copy-done((bf16[768,768]{1,0:T(8,128)(2,1)S(1)}, bf16[768,768]{1,0:T(8,128)(2,1)}, u32[]{:S(2)}) %copy-start.1) | copy-done | bytes 1179672
  7.0 0.0 copy-start.2
  7.0 1.1 %copy-done.2 = bf16[1536,256]{1,0:T(8,128)(2,1)S(1)} copy-done((bf16[1536,256]{1,0:T(8,128)(2,1)S(1)}, bf16[1536,256]{1,0:T(8,128)(2,1)}, u32[]{:S(2)}) %copy-start.2) | copy-done | bytes 786456
  8.2 0.0 copy-start.3
  8.2 0.9 %copy-done.3 = bf16[64,768]{1,0:T(8,128)(2,1)S(1)} copy-done((bf16[64,768]{1,0:T(8,128)(2,1)S(1)}, bf16[64,768]{1,0:T(8,128)(2,1)}, u32[]{:S(2)}) %copy-start.3) | copy-done | bytes 98328
  9.1 0.0 copy-start.4
  9.1 0.8 %copy-done.4 = s32[8192]{0:T(1024)S(1)} copy-done((s32[8192]{0:T(1024)S(1)}, s32[8192]{0:T(1024)}, u32[]{:S(2)}) %copy-start.4) | copy-done | bytes 32792
  9.8 0.0 copy-start.5
  9.8 0.7 %copy-done.5 = f32[128]{0:T(128)S(1)} copy-done((f32[128]{0:T(128)S(1)}, f32[128]{0:T(128)}, u32[]{:S(2)}) %copy-start.5) | copy-done | bytes 536
  10.5 19.6 %shard_map.113 = (bf16[256,768]{1,0:T(8,128)(2,1)S(1)}, f32[128,64]{1,0:T(8,128)S(1)}) custom-call(s32[64,128]{1,0:T(8,128)S(1)} %bitcast.9, bf16[64,768]{1,0:T(8,128)(2,1)S(1)} %copy-done.3, f32[1,768]{1,0:T(1,128)S(1)} %broadcast_in_dim.9.conv_gain, bf16[3,768,384]{2,1,0:T(8,128)(2,1)S(1)} %copy-done, bf16[768,768]{1,0:T(8,128)(2,1)S(1)} %copy-done.1, ...), custom_call_target="tpu_custom_call" | custom-call | tf_op jit(solution)/shard_map/pallas_call | solution.py:468
  30.1 0.6 %convert_element_type.3 = bf16[128,64]{1,0:T(8,128)(2,1)} convert(f32[128,64]{1,0:T(8,128)S(1)} %get-tuple-element.5) | non-fusion elementwise | flops 8192 | bytes 49152 | tf_op jit(solution)/shard_map/convert_element_type | solution.py:528
  30.8 0.7 %copy.15 = bf16[256,768]{1,0:T(8,128)(2,1)} copy(bf16[256,768]{1,0:T(8,128)(2,1)S(1)} %get-tuple-element.8) | data formatting | bytes 786432
Async XLA Ops:
  4.3 1.5 %copy-start = (bf16[3,768,384]{2,1,0:T(8,128)(2,1)S(1)}, bf16[3,768,384]{2,1,0:T(8,128)(2,1)}, u32[]{:S(2)}) copy-start(bf16[3,768,384]{2,1,0:T(8,128)(2,1)} %dilated_weight.1) | copy-start | bytes 5308420
  5.8 1.3 %copy-start.1 = (bf16[768,768]{1,0:T(8,128)(2,1)S(1)}, bf16[768,768]{1,0:T(8,128)(2,1)}, u32[]{:S(2)}) copy-start(bf16[768,768]{1,0:T(8,128)(2,1)} %widen_weight.1) | copy-start | bytes 3538948
  7.0 1.1 %copy-start.2 = (bf16[1536,256]{1,0:T(8,128)(2,1)S(1)}, bf16[1536,256]{1,0:T(8,128)(2,1)}, u32[]{:S(2)}) copy-start(bf16[1536,256]{1,0:T(8,128)(2,1)} %proj_weight.1) | copy-start | bytes 2359300
  8.2 0.9 %copy-start.3 = (bf16[64,768]{1,0:T(8,128)(2,1)S(1)}, bf16[64,768]{1,0:T(8,128)(2,1)}, u32[]{:S(2)}) copy-start(bf16[64,768]{1,0:T(8,128)(2,1)} %stem_weight.1) | copy-start | bytes 294916
  9.1 0.8 %copy-start.4 = (s32[8192]{0:T(1024)S(1)}, s32[8192]{0:T(1024)}, u32[]{:S(2)}) copy-start(s32[8192]{0:T(1024)} %param.10) | copy-start | bytes 98308
  9.8 0.7 %copy-start.5 = (f32[128]{0:T(128)S(1)}, f32[128]{0:T(128)}, u32[]{:S(2)}) copy-start(f32[128]{0:T(128)} %param.17) | copy-start | bytes 1540

commit v2 on v1

--- a/solution.py
+++ b/solution.py
@@ -32,6 +32,21 @@
 
 def dot(a, b):
     return jnp.dot(a, b, preferred_element_type=f32)
+
+
+def pair_conv(act, weight, height, width):
+    total = None
+    for a in range(3):
+        for b in range(3):
+            window = act[a : a + height, b : b + width, :].reshape(height * width, act.shape[2])
+            term = lax.dot_general(
+                window.astype(bf16),
+                weight[3 * a + b],
+                (((1,), (1,)), ((), ())),
+                preferred_element_type=f32,
+            )
+            total = term if total is None else total + term
+    return total
 
 
 def kernel(
@@ -110,6 +125,9 @@
         else:
             lax.fori_loop(1, count, lambda d, c: (body(d), c)[1], 0)
 
+    pc_own = pair_one.shape[1]
+    own_out = pl.ds(pl.multiple_of(chan * pc_own, pc_own), pc_own)
+    other_out = pl.ds(pl.multiple_of(other * pc_own, pc_own), pc_own)
     pairs = [
         (codes, codes_ext.at[pl.ds(8, code_rows)]),
         (stem_weight, stem_w),
@@ -119,7 +137,7 @@
         (token_gain, tgain_w),
         (proj_weight, proj_w),
         (dist_weight, dist_w),
-        (pair_one, one_w.at[chan]),
+        (pair_one, one_w.at[:, own_out]),
         (pair_two, two_w),
     ]
     loads = [pltpu.make_async_copy(a, b, load_sem.at[i]) for i, (a, b) in enumerate(pairs)]
@@ -135,6 +153,20 @@
         pl.semaphore_signal(barrier, inc=1, device_id=place(peer), device_id_type=MESH)
 
     each_peer(greet)
+    row_anchor, col_anchor = seq * tile_h, section * tile_w
+    row_fac[...] = jnp.zeros_like(row_fac)
+    col_fac[...] = jnp.zeros_like(col_fac)
+    l_dist.wait()
+    weight = dist_w[...]
+    col_index = col_anchor - 2 + iota((start_w, pc), 0)
+
+    def distance(i, carry):
+        gap = jnp.abs(col_index - (row_anchor - 2 + i)).astype(f32)
+        dist_scr[i] = jnp.log1p(gap) / math.log(total) * weight
+        return carry
+
+    lax.fori_loop(0, start_h, distance, 0)
+
     pl.semaphore_wait(barrier, count)
 
     to_next = pltpu.make_async_remote_copy(
@@ -155,7 +187,7 @@
     )
     one_copy = pltpu.make_async_remote_copy(
         src_ref=pair_one,
-        dst_ref=one_w.at[chan],
+        dst_ref=one_w.at[:, own_out],
         send_sem=one_send,
         recv_sem=one_recv,
         device_id={"chan": other},
@@ -163,7 +195,7 @@
     )
     one_in = pltpu.make_async_remote_copy(
         src_ref=pair_one,
-        dst_ref=one_w.at[other],
+        dst_ref=one_w.at[:, other_out],
         send_sem=one_send,
         recv_sem=one_recv,
         device_id={"chan": other},
@@ -181,132 +213,145 @@
 
     one_copy.start()
 
-    row_anchor, col_anchor = seq * tile_h, section * tile_w
-    row_fac[...] = jnp.zeros_like(row_fac)
-    col_fac[...] = jnp.zeros_like(col_fac)
-    l_dist.wait()
-    weight = dist_w[...]
-    col_index = col_anchor - 2 + iota((start_w, pc), 0)
-    for i in range(start_h):
-        gap = jnp.abs(col_index - (row_anchor - 2 + i)).astype(f32)
-        dist_scr[i] = jnp.log1p(gap) / math.log(total) * weight
-
-    @pl.when(first)
-    def _():
-        codes_ext[pl.ds(0, 8), :] = jnp.zeros((8, codes_ext.shape[1]), jnp.int32)
-
-    @pl.when(jnp.logical_not(first))
-    def _():
-        to_next.wait_recv()
-
-    @pl.when(last)
-    def _():
-        codes_ext[pl.ds(8 + code_rows, 8), :] = jnp.zeros((8, codes_ext.shape[1]), jnp.int32)
-
-    @pl.when(jnp.logical_not(last))
-    def _():
-        to_prev.wait_recv()
-
-    l_codes.wait()
     reach = DILATION_ROWS // 2
     ext = norm_scr.shape[0] // 2
-    per_row = codes_ext.shape[1] // PATCH
+    lanes = codes_ext.shape[1]
+    per_row = lanes // PATCH
     shift = 8 * per_row
-
-    def patch_of(shape):
-        line = iota(shape, 0)
-        odd = (line >= ext).astype(jnp.int32)
-        return 2 * (line - ext * odd - reach) + odd
+    select = (iota((lanes, 4 * PATCH), 0) % PATCH) == (iota((lanes, 4 * PATCH), 1) // 4)
+    select = select.astype(f32).astype(bf16)
+    gain_rows = [gain_w.at[pl.ds(r, 1)] for r in range(gain_w.shape[0])]
+
+    def stem_block(line_of, height, source, low, high, store):
+        def patch_of(width):
+            line = line_of(iota((height, width), 0))
+            odd = (line >= ext).astype(jnp.int32)
+            return 2 * (line - ext * odd - reach) + odd
+
+        code_row = (patch_of(source.shape[0]) + shift) // per_row - (ext_rows - source.shape[0]) // 2
+        taken = code_row == iota((height, source.shape[0]), 1)
+        spread = dot(taken.astype(f32).astype(bf16), source.astype(f32).astype(bf16))
+        mine = (iota((height, lanes), 1) // PATCH) == ((patch_of(lanes) + shift) % per_row)
+        spread = jnp.where(mine, spread, 0.0).astype(bf16)
+        code = dot(spread, select)
+        patch = patch_of(4 * PATCH)
+        letter = (iota((height, 4 * PATCH), 1) % 4).astype(f32)
+        hit = (code == letter) & (patch >= low) & (patch < high)
+        onehot = jnp.where(hit, 1.0, 0.0).astype(bf16)
+        stem = rounded(dot(onehot, stem_w[...]))
+        square = jnp.sum(stem * stem, axis=1, keepdims=True)
+        scale = lax.rsqrt(square / (2 * own_width) + epsilon)
+        gain = jnp.concatenate([row[...] for row in gain_rows], axis=1)
+        store(stem, stem * scale * gain)
 
     ext_rows = codes_ext.shape[0]
-    lanes = codes_ext.shape[1]
-    taken = ((patch_of((2 * ext, ext_rows)) + shift) // per_row) == iota((2 * ext, ext_rows), 1)
-    spread = dot(taken.astype(f32).astype(bf16), codes_ext[...].astype(f32).astype(bf16))
-    patch = patch_of((2 * ext, lanes))
-    mine = (iota((2 * ext, lanes), 1) // PATCH) == ((patch + shift) % per_row)
-    spread = jnp.where(mine, spread, 0.0).astype(bf16)
-    select = (iota((lanes, 4 * PATCH), 0) % PATCH) == (iota((lanes, 4 * PATCH), 1) // 4)
-    code = dot(spread, select.astype(f32).astype(bf16))
-    patch = patch_of((2 * ext, 4 * PATCH))
+    tiles = 3 if (2 * ext) % 24 == 0 else 1
+    tile = 2 * ext // tiles
+    l_codes.wait()
+    l_stem.wait()
+    l_gain.wait()
+
+    def inner(t, carry):
+        start = t * tile
+        span = pl.ds(pl.multiple_of(start, 8), tile)
+
+        def store(stem, norm):
+            for part in range(2):
+                stem_scr[part, span, :] = stem[:, part * own_width : (part + 1) * own_width]
+            norm_scr[span, :] = norm
+
+        inside = codes_ext[pl.ds(8, code_rows), :]
+        stem_block(lambda line: line + start, tile, inside, 0, rows, store)
+        return carry
+
+    lax.fori_loop(0, tiles, inner, 0)
+
+    @pl.when(first)
+    def _():
+        codes_ext[pl.ds(0, 8), :] = jnp.zeros((8, codes_ext.shape[1]), jnp.int32)
+
+    @pl.when(jnp.logical_not(first))
+    def _():
+        to_next.wait_recv()
+
+    @pl.when(last)
+    def _():
+        codes_ext[pl.ds(8 + code_rows, 8), :] = jnp.zeros((8, codes_ext.shape[1]), jnp.int32)
+
+    @pl.when(jnp.logical_not(last))
+    def _():
+        to_prev.wait_recv()
+
+    def edge_line(line):
+        block = line // 8
+        return line % 8 + (block % 2) * (ext - 8) + (block // 2) * ext
+
+    def edge_store(stem, norm):
+        for block in range(4):
+            at = (block % 2) * (ext - 8) + (block // 2) * ext
+            norm_scr[at : at + 8, :] = norm[8 * block : 8 * block + 8]
+
     low = jnp.where(first, 0, -shift)
     high = jnp.where(last, rows, rows + shift)
-    letter = (iota((2 * ext, 4 * PATCH), 1) % 4).astype(f32)
-    hit = (code == letter) & (patch >= low) & (patch < high)
-    onehot = jnp.where(hit, 1.0, 0.0).astype(bf16)
-
-    l_stem.wait()
-    l_gain.wait()
-    square = jnp.zeros((2 * ext, 1), f32)
-    stems = []
-    for part in range(2):
-        stem = rounded(dot(onehot, stem_w[:, part * own_width : (part + 1) * own_width]))
-        stem_scr[part] = stem
-        stems.append(stem)
-        square = square + jnp.sum(stem * stem, axis=1, keepdims=True)
-    scale = lax.rsqrt(square / (2 * own_width) + epsilon)
-    for part in range(2):
-        cols = slice(part * own_width, (part + 1) * own_width)
-        norm_scr[:, cols] = stems[part] * scale * gain_w[:, cols]
+    stem_block(edge_line, 32, codes_ext[...], low, high, edge_store)
 
     l_dil.wait()
     piece = half_rows // CHUNKS
-    half_copies = []
-    for c in range(CHUNKS):
-        taps = None
-        for k in range(3):
-            at = c * piece + k * reach
-            window = jnp.concatenate(
-                [norm_scr[at : at + piece, :], norm_scr[ext + at : ext + at + piece, :]], axis=0
-            ).astype(bf16)
-            term = dot(window, dil_w[k])
-            taps = term if taps is None else taps + term
-        at = c * piece + reach
-        stem_own = jnp.concatenate(
-            [stem_scr[chan, at : at + piece, :], stem_scr[chan, ext + at : ext + at + piece, :]], axis=0
-        )
-        tower = stem_own + jax.nn.gelu(taps)
-        top = jnp.maximum(tower[:piece], tower[piece:]).astype(bf16)
-        span = pl.ds(c * piece, piece)
-        halved[chan, span, :] = top
-        copy = pltpu.make_async_remote_copy(
+
+    def half_copy(c, source):
+        span = pl.ds(pl.multiple_of(c * piece, piece), piece)
+        return pltpu.make_async_remote_copy(
             src_ref=halved.at[chan, span],
-            dst_ref=halved.at[chan, span],
+            dst_ref=halved.at[source, span],
             send_sem=half_send.at[c],
             recv_sem=half_recv.at[c],
             device_id={"chan": other},
             device_id_type=MESH,
         )
-        copy.start()
-        half_copies.append(copy)
+
+    def convolve(c, carry):
+        base = c * piece
+        area = pl.ds(pl.multiple_of(base, 8), piece + 8)
+        area_odd = pl.ds(pl.multiple_of(ext + base, 8), piece + 8)
+        even, odd = norm_scr[area, :], norm_scr[area_odd, :]
+        taps = None
+        for k in range(3):
+            at = k * reach
+            window = jnp.concatenate([even[at : at + piece], odd[at : at + piece]], axis=0)
+            term = dot(window.astype(bf16), dil_w[k])
+            taps = term if taps is None else taps + term
+        even, odd = stem_scr[chan, area, :], stem_scr[chan, area_odd, :]
+        stem_own = jnp.concatenate([even[reach : reach + piece], odd[reach : reach + piece]], axis=0)
+        tower = stem_own + jax.nn.gelu(taps)
+        top = jnp.maximum(tower[:piece], tower[piece:]).astype(bf16)
+        halved[chan, pl.ds(pl.multiple_of(base, piece), piece), :] = top
+        half_copy(c, chan).start()
+        return carry
+
+    lax.fori_loop(0, CHUNKS, convolve, 0)
 
     l_wid.wait()
-    pieces = []
-    for c in range(CHUNKS):
-        span = pl.ds(c * piece, piece)
-        own_k = pl.ds(pl.multiple_of(chan * own_width, own_width), own_width)
-        other_k = pl.ds(pl.multiple_of(other * own_width, own_width), own_width)
+    own_k = pl.ds(pl.multiple_of(chan * own_width, own_width), own_width)
+    other_k = pl.ds(pl.multiple_of(other * own_width, own_width), own_width)
+    tokens[chan] = jnp.zeros(tokens.shape[1:], f32)
+    per_piece = piece // POOL
+
+    def widen(c, carry):
+        span = pl.ds(pl.multiple_of(c * piece, piece), piece)
         wide = dot(halved[chan, span, :], wid_w[own_k, :])
-        arrival = pltpu.make_async_remote_copy(
-            src_ref=halved.at[chan, span],
-            dst_ref=halved.at[other, span],
-            send_sem=half_send.at[c],
-            recv_sem=half_recv.at[c],
-            device_id={"chan": other},
-            device_id_type=MESH,
-        )
-        arrival.wait_recv()
+        half_copy(c, other).wait_recv()
         wide = wide + dot(halved[other, span, :], wid_w[other_k, :])
         feature = jax.nn.gelu(wide).astype(bf16)
         fine[span, :] = feature
         feature = feature.astype(f32)
-        for t in range(piece // POOL):
+        for t in range(per_piece):
             mean = jnp.sum(feature[t * POOL : (t + 1) * POOL], axis=0, keepdims=True) * (1.0 / POOL)
-            pieces.append(rounded(mean))
+            tokens[chan, pl.ds(c * per_piece + t, 1), :] = rounded(mean)
+        return carry
+
+    lax.fori_loop(0, CHUNKS, widen, 0)
     out_copy = pltpu.make_async_copy(fine, fine_out, out_sem)
     out_copy.start()
-    for t in range(tokens.shape[1]):
-        value = pieces[t] if t < tok_count else jnp.zeros_like(pieces[0])
-        tokens[chan, t : t + 1, :] = value
     tok_copy = pltpu.make_async_remote_copy(
         src_ref=tokens.at[chan],
         dst_ref=tokens.at[chan],
@@ -329,7 +374,8 @@
     tok_in.wait_recv()
     whole = jnp.concatenate([tokens[0], tokens[1]], axis=1)
     mean_square = jnp.sum(whole * whole, axis=1, keepdims=True) / whole.shape[1]
-    token_norm = (whole * lax.rsqrt(mean_square + epsilon) * tgain_w[...]).astype(bf16)
+    tgain = jnp.concatenate([tgain_w[r : r + 1, :] for r in range(tgain_w.shape[0])], axis=1)
+    token_norm = (whole * lax.rsqrt(mean_square + epsilon) * tgain).astype(bf16)
     factor = rounded(dot(token_norm, proj_w[...]))
     factors[pos, 0:tok_count, :] = factor[:tok_count, :pc]
     factors[pos, tok_count : 2 * tok_count, :] = factor[:tok_count, pc:]
@@ -376,13 +422,7 @@
 
     one_in.wait_recv()
     l_one.wait()
-    windows = [
-        act_scr[a : a + mid_h, b : b + mid_w, :].reshape(mid_h * mid_w, pc).astype(bf16)
-        for a in range(3)
-        for b in range(3)
-    ]
-    flat = jnp.concatenate(windows, axis=1)
-    conv = jnp.concatenate([dot(flat, one_w[0]), dot(flat, one_w[1])], axis=1)
+    conv = pair_conv(act_scr, one_w, mid_h, mid_w)
     middle = rounded(start_scr[1 : 1 + mid_h, 1 : 1 + mid_w, :].reshape(mid_h * mid_w, pc) + conv)
     mid_scr[...] = middle.reshape(mid_h, mid_w, pc)
     col_mid = col_anchor - 1 + iota((mid_w, pc), 0)
@@ -393,12 +433,7 @@
         act_two_scr[i] = jnp.where(inside, jax.nn.gelu(mid_scr[i]), 0.0)
 
     l_two.wait()
-    windows = [
-        act_two_scr[a : a + tile_h, b : b + tile_w, :].reshape(tile_h * tile_w, pc).astype(bf16)
-        for a in range(3)
-        for b in range(3)
-    ]
-    conv = dot(jnp.concatenate(windows, axis=1), two_w[...])
+    conv = pair_conv(act_two_scr, two_w, tile_h, tile_w)
     middle = mid_scr[1 : 1 + tile_h, 1 : 1 + tile_w, :].reshape(tile_h * tile_w, pc)
     width = conv.shape[1]
     own = jnp.where(chan == 0, middle[:, :width], middle[:, width:])
@@ -413,8 +448,8 @@
         to_prev.wait_send()
 
     one_copy.wait_send()
-    for copy in half_copies:
-        copy.wait_send()
+    for c in range(CHUNKS):
+        half_copy(c, chan).wait_send()
     tok_copy.wait_send()
 
     def sent(d):
@@ -459,17 +494,18 @@
     start_h, start_w = tile_h + 4, round_up(mid_w + 2, 8)
     ext = round_up(half_rows + DILATION_ROWS, 8)
     total = tok_count * count
-    one = pair_weight_one.reshape(-1, pc_own)
-    two = pair_weight_two.reshape(-1, pc_own)
-    gain, tgain, dist = conv_gain[None], token_gain[None], dist_weight[None]
+    one = pair_weight_one.transpose(0, 1, 3, 2).reshape(-1, pc_own, pc)
+    two = pair_weight_two.transpose(0, 1, 3, 2).reshape(-1, pc_own, pc)
+    gain, tgain = conv_gain.reshape(-1, lanes), token_gain.reshape(-1, lanes)
+    dist = dist_weight[None]
     dma = pltpu.SemaphoreType.DMA
-    anywhere = pl.BlockSpec(memory_space=pl.ANY)
+    anywhere = pl.BlockSpec(memory_space=pltpu.HBM)
     vmem = pltpu.VMEM
     fine, pair = pl.pallas_call(
         functools.partial(kernel, n_seq, n_sec),
         out_shape=(
             jax.ShapeDtypeStruct((half_rows, wide), bf16),
-            jax.ShapeDtypeStruct((tile_h * tile_w, pc_own), f32),
+            jax.ShapeDtypeStruct((tile_h * tile_w, pc_own), bf16),
         ),
         in_specs=[anywhere] * 10,
         out_specs=(anywhere, pl.BlockSpec(memory_space=pltpu.VMEM)),
@@ -482,7 +518,7 @@
             vmem(tgain.shape, f32),
             vmem(proj_weight.shape, bf16),
             vmem(dist.shape, f32),
-            vmem((2,) + one.shape, bf16),
+            vmem((one.shape[0], pc, pc), bf16),
             vmem(two.shape, bf16),
             vmem((2, 2 * ext, own_width), f32),
             vmem((2 * ext, channels), f32),
@@ -511,7 +547,7 @@
             dma,
         ],
         compiler_params=pltpu.CompilerParams(
-            collective_id=0, has_side_effects=True, vmem_limit_bytes=48 * 1024 * 1024
+            collective_id=0, has_side_effects=True, vmem_limit_bytes=64 * 1024 * 1024 - 65536
         ),
     )(
         codes,
@@ -525,7 +561,7 @@
         one,
         two,
     )
-    pair_map = pair.astype(bf16).T.reshape(pc_own, tile_h, tile_w)
+    pair_map = pair.T.reshape(pc_own, tile_h, tile_w)
     return fine, pair_map
 
 

time: 31.9 us -> 23.3 us (0.73)
  local copies, waits for them, and re-layouts: 10.6 us -> 3.14 us
  other arithmetic: 0.62 us -> 0 us
    unnamed x15 -> x2, local copies, waits for them, and re-layouts: 9.19 us -> 3.14 us
    broadcast_in_dim x2 -> x0, local copies, waits for them, and re-layouts: 1.39 us -> none  [per_device(): gain, tgain, dist = (conv_gain[None], token_gain[None], dist_weight[None])]
    convert_element_type x1 -> x0, other arithmetic: 0.62 us -> none  [per_device(): pair_map = pair.astype(bf16).T.reshape(pc_own, tile_h, tile_w)]
where the time goes in v2:
time: 23.3 us; the launch traced here: 23.1 us
  Pallas kernels  19.3 us (83%)
  local copies, waits for them, and re-layouts  3.14 us (13%)
  between operations  0.64 us (3%)
    pallas_call x1, Pallas kernels, per_device(): pl.pallas_call(functools.partial(kernel, n_seq, n_sec), out_shape=(jax.Sh...  19.3 us
    unnamed x2, local copies, waits for them, and re-layouts  3.14 us

profile of v2, /device:TPU:0, one launch (start us, length us, event | category | flops | bytes accessed | tf_op | source)
XLA Modules:
  0.0 23.1 jit_solution(14223433810113149394)
XLA Ops:
  0.6 19.3 %shard_map.113 = (bf16[256,768]{1,0:T(8,128)(2,1)}, bf16[128,64]{1,0:T(8,128)(2,1)}) custom-call(s32[64,128]{1,0:T(8,128)} %bitcast.15, bf16[64,768]{1,0:T(8,128)(2,1)} %stem_weight.1, f32[6,128]{1,0:T(8,128)} %bitcast.18, bf16[3,768,384]{2,1,0:T(8,128)(2,1)} %dilated_weight.1, bf16[768,768]{1,0:T(8,128)(2,1)} %widen_weight.1, f32[12,128]{1,0:T(8,128)} %bitcast.17, ...), custom_call_target="tpu_custom_call" | custom-call | tf_op jit(solution)/shard_map/pallas_call | solution.py:504
  20.0 1.8 %copy.14 = bf16[256,768]{1,0:T(8,128)(2,1)} copy(bf16[256,768]{1,0:T(8,128)(2,1)} %get-tuple-element.8) | data formatting | bytes 786432
  21.7 1.4 %copy.15 = bf16[64,8,16]{0,2,1:T(8,128)(2,1)} copy(bf16[64,8,16]{0,2,1:T(8,128)(2,1)} %bitcast.16) | data formatting | bytes 32768

commit v3 on v2

--- a/solution.py
+++ b/solution.py
@@ -12,6 +12,7 @@
 POOL = 64
 DILATION_ROWS = 4
 CHUNKS = 2
+LANES_A = 8
 MESH = pl.DeviceIdType.MESH
 epsilon = 1e-06
 f32 = jnp.float32
@@ -64,7 +65,8 @@
     pair_two,
     fine_out,
     pair_out,
-    codes_ext,
+    codes_own,
+    codes_halo,
     stem_w,
     gain_w,
     dil_w,
@@ -98,7 +100,6 @@
     tok_recv,
     fac_send,
     fac_recv,
-    out_sem,
 ):
     count = n_seq * n_sec
     seq, section, chan = lax.axis_index("seq"), lax.axis_index("section"), lax.axis_index("chan")
@@ -129,7 +130,7 @@
     own_out = pl.ds(pl.multiple_of(chan * pc_own, pc_own), pc_own)
     other_out = pl.ds(pl.multiple_of(other * pc_own, pc_own), pc_own)
     pairs = [
-        (codes, codes_ext.at[pl.ds(8, code_rows)]),
+        (codes, codes_own),
         (stem_weight, stem_w),
         (conv_gain, gain_w),
         (dilated_weight, dil_w),
@@ -171,7 +172,7 @@
 
     to_next = pltpu.make_async_remote_copy(
         src_ref=codes.at[pl.ds(code_rows - 8, 8)],
-        dst_ref=codes_ext.at[pl.ds(0, 8)],
+        dst_ref=codes_halo.at[0],
         send_sem=halo_send.at[0],
         recv_sem=halo_recv.at[0],
         device_id=place(lax.rem(pos + 1, count)),
@@ -179,7 +180,7 @@
     )
     to_prev = pltpu.make_async_remote_copy(
         src_ref=codes.at[pl.ds(0, 8)],
-        dst_ref=codes_ext.at[pl.ds(8 + code_rows, 8)],
+        dst_ref=codes_halo.at[1],
         send_sem=halo_send.at[1],
         recv_sem=halo_recv.at[1],
         device_id=place(lax.rem(pos + count - 1, count)),
@@ -214,61 +215,55 @@
     one_copy.start()
 
     reach = DILATION_ROWS // 2
-    ext = norm_scr.shape[0] // 2
-    lanes = codes_ext.shape[1]
+    lanes = codes_own.shape[1]
     per_row = lanes // PATCH
-    shift = 8 * per_row
-    select = (iota((lanes, 4 * PATCH), 0) % PATCH) == (iota((lanes, 4 * PATCH), 1) // 4)
-    select = select.astype(f32).astype(bf16)
-    gain_rows = [gain_w.at[pl.ds(r, 1)] for r in range(gain_w.shape[0])]
-
-    def stem_block(line_of, height, source, low, high, store):
-        def patch_of(width):
-            line = line_of(iota((height, width), 0))
-            odd = (line >= ext).astype(jnp.int32)
-            return 2 * (line - ext * odd - reach) + odd
-
-        code_row = (patch_of(source.shape[0]) + shift) // per_row - (ext_rows - source.shape[0]) // 2
-        taken = code_row == iota((height, source.shape[0]), 1)
-        spread = dot(taken.astype(f32).astype(bf16), source.astype(f32).astype(bf16))
-        mine = (iota((height, lanes), 1) // PATCH) == ((patch_of(lanes) + shift) % per_row)
-        spread = jnp.where(mine, spread, 0.0).astype(bf16)
-        code = dot(spread, select)
-        patch = patch_of(4 * PATCH)
-        letter = (iota((height, 4 * PATCH), 1) % 4).astype(f32)
-        hit = (code == letter) & (patch >= low) & (patch < high)
-        onehot = jnp.where(hit, 1.0, 0.0).astype(bf16)
-        stem = rounded(dot(onehot, stem_w[...]))
-        square = jnp.sum(stem * stem, axis=1, keepdims=True)
+    steps = per_row // 2
+    groups = code_rows // LANES_A
+    line_count = half_rows // LANES_A
+    pad = reach * LANES_A
+    ext = half_rows + 2 * pad
+    letters = 4 * PATCH
+    wide_lanes = per_row * lanes
+    source = iota((lanes, wide_lanes), 0)
+    column = iota((lanes, wide_lanes), 1)
+    wanted = (column // lanes) * PATCH + (column % lanes) // 4
+    select = ((source == wanted) & (column % lanes < letters)).astype(f32).astype(bf16)
+
+    def coded(parts):
+        picked = jnp.concatenate(parts, axis=0)
+        code = dot(picked.astype(f32).astype(bf16), select)
+        letter = (iota(code.shape, 1) % 4).astype(f32)
+        return jnp.where(code == letter, 1.0, 0.0)
+
+    def stem_lines(onehot):
+        stem = dot(onehot.astype(bf16), stem_w[...]).astype(bf16)
+        value = stem.astype(f32)
+        square = jnp.sum(value * value, axis=1, keepdims=True)
         scale = lax.rsqrt(square / (2 * own_width) + epsilon)
-        gain = jnp.concatenate([row[...] for row in gain_rows], axis=1)
-        store(stem, stem * scale * gain)
-
-    ext_rows = codes_ext.shape[0]
-    tiles = 3 if (2 * ext) % 24 == 0 else 1
-    tile = 2 * ext // tiles
+        return stem, (value * scale * gain).astype(bf16)
+
     l_codes.wait()
     l_stem.wait()
     l_gain.wait()
-
-    def inner(t, carry):
-        start = t * tile
-        span = pl.ds(pl.multiple_of(start, 8), tile)
-
-        def store(stem, norm):
-            for part in range(2):
-                stem_scr[part, span, :] = stem[:, part * own_width : (part + 1) * own_width]
-            norm_scr[span, :] = norm
-
-        inside = codes_ext[pl.ds(8, code_rows), :]
-        stem_block(lambda line: line + start, tile, inside, 0, rows, store)
-        return carry
-
-    lax.fori_loop(0, tiles, inner, 0)
+    gain = jnp.concatenate([gain_w[r : r + 1, :] for r in range(gain_w.shape[0])], axis=1)
+    own_groups = [codes_own[pl.ds(s, LANES_A, stride=groups), :] for s in range(groups)]
+    codes_hot = coded(own_groups)
+    for e in range(2):
+        blocks = []
+        for m in range(line_count):
+            group, step = m // steps, m % steps
+            at = (2 * step + e) * lanes
+            blocks.append(codes_hot[group * LANES_A : (group + 1) * LANES_A, at : at + letters])
+        stem, norm = stem_lines(jnp.concatenate(blocks, axis=0))
+        for part in range(2):
+            stem_scr[part, e * half_rows : (e + 1) * half_rows, :] = stem[
+                :, part * own_width : (part + 1) * own_width
+            ]
+        norm_scr[e * ext + pad : e * ext + pad + half_rows, :] = norm
 
     @pl.when(first)
     def _():
-        codes_ext[pl.ds(0, 8), :] = jnp.zeros((8, codes_ext.shape[1]), jnp.int32)
+        codes_halo[0] = jnp.zeros((8, lanes), jnp.int32)
 
     @pl.when(jnp.logical_not(first))
     def _():
@@ -276,24 +271,28 @@
 
     @pl.when(last)
     def _():
-        codes_ext[pl.ds(8 + code_rows, 8), :] = jnp.zeros((8, codes_ext.shape[1]), jnp.int32)
+        codes_halo[1] = jnp.zeros((8, lanes), jnp.int32)
 
     @pl.when(jnp.logical_not(last))
     def _():
         to_prev.wait_recv()
 
-    def edge_line(line):
-        block = line // 8
-        return line % 8 + (block % 2) * (ext - 8) + (block // 2) * ext
-
-    def edge_store(stem, norm):
-        for block in range(4):
-            at = (block % 2) * (ext - 8) + (block // 2) * ext
-            norm_scr[at : at + 8, :] = norm[8 * block : 8 * block + 8]
-
-    low = jnp.where(first, 0, -shift)
-    high = jnp.where(last, rows, rows + shift)
-    stem_block(edge_line, 32, codes_ext[...], low, high, edge_store)
+    before = jnp.concatenate([codes_halo[0][7:8], own_groups[groups - 1][: LANES_A - 1]], axis=0)
+    after = jnp.concatenate([own_groups[0][1:LANES_A], codes_halo[1][0:1]], axis=0)
+    codes_hot = coded([before, after])
+    line = iota(codes_hot.shape, 0)
+    outside = ((line == 0) & first) | ((line == 2 * LANES_A - 1) & last)
+    codes_hot = jnp.where(outside, 0.0, codes_hot)
+    blocks = []
+    for e in range(2):
+        for end, m_list in enumerate((range(steps - reach, steps), range(reach))):
+            for step in m_list:
+                at = (2 * step + e) * lanes
+                blocks.append(codes_hot[end * LANES_A : (end + 1) * LANES_A, at : at + letters])
+    _, norm = stem_lines(jnp.concatenate(blocks, axis=0))
+    for e in range(2):
+        norm_scr[e * ext : e * ext + pad, :] = norm[2 * e * pad : (2 * e + 1) * pad]
+        norm_scr[(e + 1) * ext - pad : (e + 1) * ext, :] = norm[(2 * e + 1) * pad : (2 * e + 2) * pad]
 
     l_dil.wait()
     piece = half_rows // CHUNKS
@@ -311,17 +310,15 @@
 
     def convolve(c, carry):
         base = c * piece
-        area = pl.ds(pl.multiple_of(base, 8), piece + 8)
-        area_odd = pl.ds(pl.multiple_of(ext + base, 8), piece + 8)
-        even, odd = norm_scr[area, :], norm_scr[area_odd, :]
-        taps = None
+        windows = []
         for k in range(3):
-            at = k * reach
-            window = jnp.concatenate([even[at : at + piece], odd[at : at + piece]], axis=0)
-            term = dot(window.astype(bf16), dil_w[k])
-            taps = term if taps is None else taps + term
-        even, odd = stem_scr[chan, area, :], stem_scr[chan, area_odd, :]
-        stem_own = jnp.concatenate([even[reach : reach + piece], odd[reach : reach + piece]], axis=0)
+            even = norm_scr[pl.ds(pl.multiple_of(base + k * pad, 16), piece), :]
+            odd = norm_scr[pl.ds(pl.multiple_of(ext + base + k * pad, 16), piece), :]
+            windows.append(jnp.concatenate([even, odd], axis=0))
+        taps = dot(jnp.concatenate(windows, axis=1), dil_w[...].reshape(-1, own_width))
+        even = stem_scr[chan, pl.ds(pl.multiple_of(base, 16), piece), :]
+        odd = stem_scr[chan, pl.ds(pl.multiple_of(half_rows + base, 16), piece), :]
+        stem_own = jnp.concatenate([even, odd], axis=0).astype(f32)
         tower = stem_own + jax.nn.gelu(taps)
         top = jnp.maximum(tower[:piece], tower[piece:]).astype(bf16)
         halved[chan, pl.ds(pl.multiple_of(base, piece), piece), :] = top
@@ -333,25 +330,23 @@
     l_wid.wait()
     own_k = pl.ds(pl.multiple_of(chan * own_width, own_width), own_width)
     other_k = pl.ds(pl.multiple_of(other * own_width, own_width), own_width)
-    tokens[chan] = jnp.zeros(tokens.shape[1:], f32)
-    per_piece = piece // POOL
-
-    def widen(c, carry):
+
+    def widen(c, sums):
         span = pl.ds(pl.multiple_of(c * piece, piece), piece)
         wide = dot(halved[chan, span, :], wid_w[own_k, :])
         half_copy(c, other).wait_recv()
         wide = wide + dot(halved[other, span, :], wid_w[other_k, :])
         feature = jax.nn.gelu(wide).astype(bf16)
         fine[span, :] = feature
-        feature = feature.astype(f32)
-        for t in range(per_piece):
-            mean = jnp.sum(feature[t * POOL : (t + 1) * POOL], axis=0, keepdims=True) * (1.0 / POOL)
-            tokens[chan, pl.ds(c * per_piece + t, 1), :] = rounded(mean)
-        return carry
-
-    lax.fori_loop(0, CHUNKS, widen, 0)
-    out_copy = pltpu.make_async_copy(fine, fine_out, out_sem)
-    out_copy.start()
+        stacked = feature.astype(f32).reshape(piece // LANES_A, LANES_A, feature.shape[1])
+        return sums + jnp.sum(stacked, axis=0)
+
+    sums = lax.fori_loop(0, CHUNKS, widen, jnp.zeros((LANES_A, fine.shape[1]), f32))
+    per_token = LANES_A // tok_count
+    tokens[chan] = jnp.zeros(tokens.shape[1:], f32)
+    for t in range(tok_count):
+        mean = jnp.sum(sums[t * per_token : (t + 1) * per_token], axis=0, keepdims=True) * (1.0 / POOL)
+        tokens[chan, t : t + 1, :] = rounded(mean)
     tok_copy = pltpu.make_async_remote_copy(
         src_ref=tokens.at[chan],
         dst_ref=tokens.at[chan],
@@ -361,6 +356,10 @@
         device_id_type=MESH,
     )
     tok_copy.start()
+    natural = iota((half_rows, half_rows), 0)
+    position = LANES_A * (natural % line_count) + natural // line_count
+    order = (position == iota((half_rows, half_rows), 1)).astype(f32).astype(bf16)
+    fine_out[...] = dot(order, fine[...]).astype(bf16)
     l_tgain.wait()
     l_proj.wait()
     tok_in = pltpu.make_async_remote_copy(
@@ -463,7 +462,6 @@
         ).wait_send()
 
     each_peer(sent)
-    out_copy.wait()
 
 
 def per_device(
@@ -492,7 +490,7 @@
     tile_h, tile_w = tok_count * n_sec, tok_count * n_seq
     mid_h, mid_w = tile_h + 2, round_up(tile_w + 2, 8)
     start_h, start_w = tile_h + 4, round_up(mid_w + 2, 8)
-    ext = round_up(half_rows + DILATION_ROWS, 8)
+    ext = half_rows + DILATION_ROWS * LANES_A
     total = tok_count * count
     one = pair_weight_one.transpose(0, 1, 3, 2).reshape(-1, pc_own, pc)
     two = pair_weight_two.transpose(0, 1, 3, 2).reshape(-1, pc_own, pc)
@@ -508,9 +506,10 @@
             jax.ShapeDtypeStruct((tile_h * tile_w, pc_own), bf16),
         ),
         in_specs=[anywhere] * 10,
-        out_specs=(anywhere, pl.BlockSpec(memory_space=pltpu.VMEM)),
+        out_specs=(pl.BlockSpec(memory_space=pltpu.VMEM),) * 2,
         scratch_shapes=[
-            vmem((codes.shape[0] + 16, lanes), jnp.int32),
+            vmem(codes.shape, jnp.int32),
+            vmem((2, 8, lanes), jnp.int32),
             vmem(stem_weight.shape, bf16),
             vmem(gain.shape, f32),
             vmem(dilated_conv_weight.shape, bf16),
@@ -520,8 +519,8 @@
             vmem(dist.shape, f32),
             vmem((one.shape[0], pc, pc), bf16),
             vmem(two.shape, bf16),
-            vmem((2, 2 * ext, own_width), f32),
-            vmem((2 * ext, channels), f32),
+            vmem((2, 2 * half_rows, own_width), bf16),
+            vmem((2 * ext, channels), bf16),
             vmem((2, half_rows, own_width), bf16),
             vmem((half_rows, wide), bf16),
             vmem((2, round_up(tok_count, 8), wide), f32),
@@ -544,22 +543,26 @@
             dma,
             dma((count,)),
             dma((count,)),
-            dma,
         ],
         compiler_params=pltpu.CompilerParams(
-            collective_id=0, has_side_effects=True, vmem_limit_bytes=64 * 1024 * 1024 - 65536
+            collective_id=0, has_side_effects=True, vmem_limit_bytes=48 * 1024 * 1024
         ),
     )(
-        codes,
-        stem_weight,
-        gain,
-        dilated_conv_weight,
-        widen_weight,
-        tgain,
-        proj_weight,
-        dist,
-        one,
-        two,
+        *(
+            pltpu.with_memory_space_constraint(operand, pltpu.HBM)
+            for operand in (
+                codes,
+                stem_weight,
+                gain,
+                dilated_conv_weight,
+                widen_weight,
+                tgain,
+                proj_weight,
+                dist,
+                one,
+                two,
+            )
+        )
     )
     pair_map = pair.T.reshape(pc_own, tile_h, tile_w)
     return fine, pair_map

time: 23.3 us -> 20.8 us (0.89)
  local copies, waits for them, and re-layouts: 3.14 us -> 1.36 us
  Pallas kernels: 19.3 us -> 18.7 us
    unnamed x2, local copies, waits for them, and re-layouts: 3.14 us -> 1.36 us
    pallas_call x1, Pallas kernels: 19.3 us -> 18.7 us  [per_device(): pl.pallas_call(functools.partial(kernel, n_seq, n_sec), out_shape=(jax.Sh...]
where the time goes in v3:
time: 20.8 us; the launch traced here: 20.7 us
  Pallas kernels  18.7 us (90%)
  local copies, waits for them, and re-layouts  1.36 us (7%)
  between operations  0.64 us (3%)
    pallas_call x1, Pallas kernels, per_device(): pl.pallas_call(functools.partial(kernel, n_seq, n_sec), out_shape=(jax.Sh...  18.7 us
    unnamed x2, local copies, waits for them, and re-layouts  1.36 us

profile of v3, /device:TPU:0, one launch (start us, length us, event | category | flops | bytes accessed | tf_op | source)
XLA Modules:
  0.0 20.7 jit_solution(6852488510659285186)
XLA Ops:
  0.6 18.7 %shard_map.113 = (bf16[256,768]{1,0:T(8,128)(2,1)S(1)}, bf16[128,64]{1,0:T(8,128)(2,1)S(1)}) custom-call(s32[64,128]{1,0:T(8,128)} %bitcast.16, bf16[64,768]{1,0:T(8,128)(2,1)} %stem_weight.1, f32[6,128]{1,0:T(8,128)} %bitcast.18, bf16[3,768,384]{2,1,0:T(8,128)(2,1)} %dilated_weight.1, bf16[768,768]{1,0:T(8,128)(2,1)} %widen_weight.1, f32[12,128]{1,0:T(8,128)} %bitcast.17, ...), custom_call_target="tpu_custom_call" | custom-call | tf_op jit(solution)/shard_map/pallas_call | solution.py:502
  19.3 0.7 %copy.14 = bf16[256,768]{1,0:T(8,128)(2,1)} copy(bf16[256,768]{1,0:T(8,128)(2,1)S(1)} %get-tuple-element.8) | data formatting | bytes 786432
  20.0 0.6 %copy.15 = bf16[64,8,16]{0,2,1:T(8,128)(2,1)} copy(bf16[64,8,16]{0,2,1:T(8,128)(2,1)S(1)} %bitcast.13) | data formatting | bytes 32768

commit v4 on v3

--- a/solution.py
+++ b/solution.py
@@ -36,18 +36,18 @@
 
 
 def pair_conv(act, weight, height, width):
-    total = None
-    for a in range(3):
-        for b in range(3):
-            window = act[a : a + height, b : b + width, :].reshape(height * width, act.shape[2])
-            term = lax.dot_general(
-                window.astype(bf16),
-                weight[3 * a + b],
-                (((1,), (1,)), ((), ())),
-                preferred_element_type=f32,
-            )
-            total = term if total is None else total + term
-    return total
+    windows = [
+        act[a : a + height, b : b + width, :].reshape(height * width, act.shape[2]).astype(bf16)
+        for a in range(3)
+        for b in range(3)
+    ]
+    taps = [weight[k] for k in range(9)]
+    return lax.dot_general(
+        jnp.concatenate(windows, axis=1),
+        jnp.concatenate(taps, axis=1),
+        (((1,), (1,)), ((), ())),
+        preferred_element_type=f32,
+    )
 
 
 def kernel(
@@ -121,7 +121,7 @@
 
     def each_peer(body):
         if count <= 16:
-            for d in range(1, count):
+            for d in sorted(range(1, count), key=lambda d: -min(d, count - d)):
                 body(d)
         else:
             lax.fori_loop(1, count, lambda d, c: (body(d), c)[1], 0)
@@ -143,9 +143,6 @@
     ]
     loads = [pltpu.make_async_copy(a, b, load_sem.at[i]) for i, (a, b) in enumerate(pairs)]
     l_codes, l_stem, l_gain, l_dil, l_wid, l_tgain, l_proj, l_dist, l_one, l_two = loads
-    for load in loads:
-        load.start()
-
     barrier = pltpu.get_barrier_semaphore()
     pl.semaphore_signal(barrier, inc=1, device_id={"chan": other}, device_id_type=MESH)
 
@@ -154,19 +151,8 @@
         pl.semaphore_signal(barrier, inc=1, device_id=place(peer), device_id_type=MESH)
 
     each_peer(greet)
-    row_anchor, col_anchor = seq * tile_h, section * tile_w
-    row_fac[...] = jnp.zeros_like(row_fac)
-    col_fac[...] = jnp.zeros_like(col_fac)
-    l_dist.wait()
-    weight = dist_w[...]
-    col_index = col_anchor - 2 + iota((start_w, pc), 0)
-
-    def distance(i, carry):
-        gap = jnp.abs(col_index - (row_anchor - 2 + i)).astype(f32)
-        dist_scr[i] = jnp.log1p(gap) / math.log(total) * weight
-        return carry
-
-    lax.fori_loop(0, start_h, distance, 0)
+    for load in loads:
+        load.start()
 
     pl.semaphore_wait(barrier, count)
 
@@ -391,6 +377,20 @@
         ).start()
 
     each_peer(send_factor)
+    row_anchor, col_anchor = seq * tile_h, section * tile_w
+    row_fac[...] = jnp.zeros_like(row_fac)
+    col_fac[...] = jnp.zeros_like(col_fac)
+    l_dist.wait()
+    weight = dist_w[...]
+    col_index = col_anchor - 2 + iota((start_w, pc), 0)
+
+    def distance(i, carry):
+        gap = jnp.abs(col_index - (row_anchor - 2 + i)).astype(f32)
+        dist_scr[i] = jnp.log1p(gap) / math.log(total) * weight
+        return carry
+
+    lax.fori_loop(0, start_h, distance, 0)
+
 
     def take_factor(d):
         source = lax.rem(pos + count - d, count)

time: 20.8 us -> 20.2 us (0.971)
  Pallas kernels: 18.7 us -> 18.1 us
    pallas_call x1, Pallas kernels: 18.7 us -> 18.1 us  [per_device(): pl.pallas_call(functools.partial(kernel, n_seq, n_sec), out_shape=(jax.Sh...]
where the time goes in v4:
time: 20.2 us; the launch traced here: 20.1 us
  Pallas kernels  18.1 us (90%)
  local copies, waits for them, and re-layouts  1.36 us (7%)
  between operations  0.64 us (3%)
    pallas_call x1, Pallas kernels, per_device(): pl.pallas_call(functools.partial(kernel, n_seq, n_sec), out_shape=(jax.Sh...  18.1 us
    unnamed x2, local copies, waits for them, and re-layouts  1.36 us

profile of v4, /device:TPU:0, one launch (start us, length us, event | category | flops | bytes accessed | tf_op | source)
XLA Modules:
  0.0 20.1 jit_solution(998747775403821620)
XLA Ops:
  0.6 18.1 %shard_map.113 = (bf16[256,768]{1,0:T(8,128)(2,1)S(1)}, bf16[128,64]{1,0:T(8,128)(2,1)S(1)}) custom-call(s32[64,128]{1,0:T(8,128)} %bitcast.16, bf16[64,768]{1,0:T(8,128)(2,1)} %stem_weight.1, f32[6,128]{1,0:T(8,128)} %bitcast.18, bf16[3,768,384]{2,1,0:T(8,128)(2,1)} %dilated_weight.1, bf16[768,768]{1,0:T(8,128)(2,1)} %widen_weight.1, f32[12,128]{1,0:T(8,128)} %bitcast.17, ...), custom_call_target="tpu_custom_call" | custom-call | tf_op jit(solution)/shard_map/pallas_call | solution.py:502
  18.7 0.7 %copy.14 = bf16[256,768]{1,0:T(8,128)(2,1)} copy(bf16[256,768]{1,0:T(8,128)(2,1)S(1)} %get-tuple-element.8) | data formatting | bytes 786432
  19.5 0.6 %copy.15 = bf16[64,8,16]{0,2,1:T(8,128)(2,1)} copy(bf16[64,8,16]{0,2,1:T(8,128)(2,1)S(1)} %bitcast.13) | data formatting | bytes 32768

commit v5 on v4

--- a/solution.py
+++ b/solution.py
@@ -381,15 +381,10 @@
     row_fac[...] = jnp.zeros_like(row_fac)
     col_fac[...] = jnp.zeros_like(col_fac)
     l_dist.wait()
-    weight = dist_w[...]
+    offset = iota(dist_scr.shape, 0) - (start_h - 1)
+    gap = jnp.abs(offset + (col_anchor - row_anchor)).astype(f32)
+    dist_scr[...] = jnp.log1p(gap) / math.log(total) * dist_w[...]
     col_index = col_anchor - 2 + iota((start_w, pc), 0)
-
-    def distance(i, carry):
-        gap = jnp.abs(col_index - (row_anchor - 2 + i)).astype(f32)
-        dist_scr[i] = jnp.log1p(gap) / math.log(total) * weight
-        return carry
-
-    lax.fori_loop(0, start_h, distance, 0)
 
 
     def take_factor(d):
@@ -413,7 +408,7 @@
     col_in = (col_index >= 0) & (col_index < total)
     for i in range(start_h):
         row_here = row_fac[pl.ds(row_anchor + 6 + i, 1), :]
-        begin = rounded(row_here * near + dist_scr[i])
+        begin = rounded(row_here * near + dist_scr[start_h - 1 - i : start_h - 1 - i + start_w, :])
         start_scr[i] = begin
         row_index = jnp.zeros_like(col_index) + (row_anchor - 2 + i)
         inside = col_in & (row_index >= 0) & (row_index < total)
@@ -462,6 +457,15 @@
         ).wait_send()
 
     each_peer(sent)
+
+
+def write_out(fine, pair, fine_out, pair_out, sems):
+    first = pltpu.make_async_copy(fine, fine_out, sems.at[0])
+    second = pltpu.make_async_copy(pair, pair_out, sems.at[1])
+    first.start()
+    second.start()
+    first.wait()
+    second.wait()
 
 
 def per_device(
@@ -527,7 +531,7 @@
             vmem((count, 2 * tok_count, pc), f32),
             vmem((total + start_h + 16, pc), f32),
             vmem((total + start_w + 16, pc), f32),
-            vmem((start_h, start_w, pc), f32),
+            vmem((start_h + start_w, pc), f32),
             vmem((start_h, start_w, pc), f32),
             vmem((start_h, start_w, pc), f32),
             vmem((mid_h, mid_w, pc), f32),
@@ -564,6 +568,16 @@
             )
         )
     )
+    fine, pair = pl.pallas_call(
+        write_out,
+        out_shape=(
+            jax.ShapeDtypeStruct(fine.shape, bf16),
+            jax.ShapeDtypeStruct(pair.shape, bf16),
+        ),
+        in_specs=[pl.BlockSpec(memory_space=pl.ANY)] * 2,
+        out_specs=(anywhere,) * 2,
+        scratch_shapes=[dma((2,))],
+    )(fine, pair)
     pair_map = pair.T.reshape(pc_own, tile_h, tile_w)
     return fine, pair_map
 

time: 20.2 us -> 34.2 us (1.69)
  Pallas kernels: 18.1 us -> 32.1 us
    pallas_call x0 -> x1, Pallas kernels: none -> 14 us  [per_device(): pl.pallas_call(write_out, out_shape=(jax.ShapeDtypeStruct(fine.shape, bf1...]
    unnamed x2 -> x4, local copies, waits for them, and re-layouts: 1.36 us -> 1.35 us
where the time goes in v5:
time: 34.2 us; the launch traced here: 34.1 us
  Pallas kernels  32.1 us (94%)
  local copies, waits for them, and re-layouts  1.35 us (4%)
  between operations  0.65 us (2%)
    pallas_call x1, Pallas kernels, per_device(): pl.pallas_call(functools.partial(kernel, n_seq, n_sec), out_shape=(jax.Sh...  18.1 us
    pallas_call x1, Pallas kernels, per_device(): pl.pallas_call(write_out, out_shape=(jax.ShapeDtypeStruct(fine.shape, bf1...  14 us
    unnamed x4, local copies, waits for them, and re-layouts  1.35 us

profile of v5, /device:TPU:0, one launch (start us, length us, event | category | flops | bytes accessed | tf_op | source)
XLA Modules:
  0.0 34.1 jit_solution(15364187501708717061)
XLA Ops:
  0.6 18.1 %shard_map.113 = (bf16[256,768]{1,0:T(8,128)(2,1)S(1)}, bf16[128,64]{1,0:T(8,128)(2,1)S(1)}) custom-call(s32[64,128]{1,0:T(8,128)} %bitcast.15, bf16[64,768]{1,0:T(8,128)(2,1)} %stem_weight.1, f32[6,128]{1,0:T(8,128)} %bitcast.17, bf16[3,768,384]{2,1,0:T(8,128)(2,1)} %dilated_weight.1, bf16[768,768]{1,0:T(8,128)(2,1)} %widen_weight.1, f32[12,128]{1,0:T(8,128)} %bitcast.16, ...), custom_call_target="tpu_custom_call" | custom-call | tf_op jit(solution)/shard_map/pallas_call | solution.py:506
  18.7 0.0 copy-start
  18.7 0.7 %copy-done = bf16[256,768]{1,0:T(8,128)(2,1)} copy-done((bf16[256,768]{1,0:T(8,128)(2,1)}, bf16[256,768]{1,0:T(8,128)(2,1)S(1)}, u32[]{:S(2)}) %copy-start) | copy-done | bytes 393240
  19.5 0.0 copy-start.1
  19.5 0.6 %copy-done.1 = bf16[128,64]{1,0:T(8,128)(2,1)} copy-done((bf16[128,64]{1,0:T(8,128)(2,1)}, bf16[128,64]{1,0:T(8,128)(2,1)S(1)}, u32[]{:S(2)}) %copy-start.1) | copy-done | bytes 16408
  20.1 14.0 %shard_map.114 = (bf16[256,768]{1,0:T(8,128)(2,1)}, bf16[128,64]{1,0:T(8,128)(2,1)}) custom-call(bf16[256,768]{1,0:T(8,128)(2,1)} %copy-done, bf16[128,64]{1,0:T(8,128)(2,1)} %copy-done.1), custom_call_target="tpu_custom_call" | custom-call | tf_op jit(solution)/shard_map/pallas_call | solution.py:571
Async XLA Ops:
  18.7 0.8 %copy-start = (bf16[256,768]{1,0:T(8,128)(2,1)}, bf16[256,768]{1,0:T(8,128)(2,1)S(1)}, u32[]{:S(2)}) copy-start(bf16[256,768]{1,0:T(8,128)(2,1)S(1)} %get-tuple-element.6.fine) | copy-start | bytes 1179652
  19.5 0.6 %copy-start.1 = (bf16[128,64]{1,0:T(8,128)(2,1)}, bf16[128,64]{1,0:T(8,128)(2,1)S(1)}, u32[]{:S(2)}) copy-start(bf16[128,64]{1,0:T(8,128)(2,1)S(1)} %get-tuple-element.7.pair) | copy-start | bytes 49156
